TPU v7x, 128 devices: a whole 4x4x4 slice. The times are simulated.
128 devices in a mesh: kv: 16 (over x, z), ep: 8 (over y, core).
Axes of the slice: x: 4, y: 4, z: 4, core: 2. Of those that a mesh axis runs over, the one named last changes fastest.
Arguments:
- queries: bfloat16 [64, 128, 576], P('ep'), may hold values from -64 to 64
- latent_cache: bfloat16 [64, 16384, 576], P('ep', 'kv'), may hold values from -7 to 7
- lengths: int32 [64], P('ep'), may hold values from 2 to 16384, as said below
- value_up: bfloat16 [128, 512, 128], P('kv'), may hold values from -6 to 6
- out_proj: bfloat16 [16384, 7168], P('kv', 'ep'), may hold values from -0.046875 to 0.046875
- residual: bfloat16 [64, 7168], P('kv', 'ep'), may hold values from -6 to 6
- norm_gain: float32 [7168], replicated, may hold values from 0.5 to 1.5
- route_ids: int32 [64, 8], replicated, may hold values from 0 to 15, all different within a row; in each aligned block of 64 rows (0 to 63, 64 to 127, ...) at most 48 rows name the same one
- route_gates: float32 [64, 8], replicated, may hold values from 0.1 to 1
- gate_weight: bfloat16 [16, 7168, 2048], P('kv', None, 'ep'), may hold values from -0.0625 to 0.0625
- up_weight: bfloat16 [16, 7168, 2048], P('kv', None, 'ep'), may hold values from -0.0625 to 0.0625
- down_weight: bfloat16 [16, 2048, 7168], P('kv', 'ep'), may hold values from -0.125 to 0.125
Outputs:
- attended: bfloat16 [64, 7168], P('kv', 'ep')
- expert_out: bfloat16 [64, 7168], P('kv', 'ep')
Inputs may be any that keep to these rules, and one draw needn't show every extreme that they name: `lengths`: some row has the full length 16384. `route_ids`: the 8 experts of a row differ; no expert is chosen by more than 48 rows, a bound that some block reaches.
All inputs are finite; a program needn't handle non-finite values.
Results may differ from a plain program's by a relative error of at most 0.025.
Values may be sent and summed in bfloat16 or wider, within the bound.
No kernel may reach another device: no remote copies, remote signals or barrier semaphores. Data moves between devices by JAX's collectives and lax.ppermute only.
A program may use at most 128 MiB of HBM per device.

v0:
```python
import jax
import jax.numpy as jnp
from jax import lax
from jax.sharding import PartitionSpec as P

SCORE_SCALE = 0.07216878364870323
NEG_FILL = -1e30
NORM_EPS = 1e-06


def on_device(
    queries,
    latent_cache,
    lengths,
    value_up,
    out_proj,
    residual,
    norm_gain,
    route_ids,
    route_gates,
    gate_weight,
    up_weight,
    down_weight,
):
    kv_count = lax.axis_size("kv")
    kv_pos = lax.axis_index("kv")
    row_count, ctx_len, unused_width = latent_cache.shape
    head_count = queries.shape[1]
    lat_width = value_up.shape[1]
    scores = (
        jnp.einsum("bhc,btc->bht", queries, latent_cache, preferred_element_type=jnp.float32)
        * SCORE_SCALE
    )
    position = kv_pos * ctx_len + jnp.arange(ctx_len, dtype=jnp.int32)
    allowed = position[None, None, :] < lengths[:, None, None]
    masked = jnp.where(allowed, scores, NEG_FILL)
    block_max = jnp.max(masked, axis=2)
    exp_terms = jnp.where(allowed, jnp.exp(masked - block_max[:, :, None]), 0.0)
    block_sum = jnp.sum(exp_terms, axis=2)
    block_out = jnp.einsum(
        "bht,btc->bhc",
        exp_terms.astype(jnp.bfloat16),
        latent_cache[:, :, :lat_width],
        preferred_element_type=jnp.float32,
    )
    received = (
        lax.all_to_all(block_out[None], "kv", split_axis=2, concat_axis=0, tiled=True),
        lax.all_to_all(block_max[None], "kv", split_axis=2, concat_axis=0, tiled=True),
        lax.all_to_all(block_sum[None], "kv", split_axis=2, concat_axis=0, tiled=True),
    )
    outs_all, max_all, sum_all = received
    highest = jnp.max(max_all, axis=0)
    factor = jnp.exp(max_all - highest[None])
    denominator = jnp.sum(factor * sum_all, axis=0)
    merged = jnp.sum(factor[..., None] * outs_all, axis=0)
    attention = (merged / denominator[..., None]).astype(jnp.bfloat16)
    head_local = head_count // kv_count
    head_values = jnp.einsum(
        "bhc,hcv->bhv", attention, value_up, preferred_element_type=jnp.float32
    )
    head_values = head_values.astype(jnp.bfloat16).reshape(
        row_count, head_local * value_up.shape[2]
    )
    all_values = lax.all_gather(head_values, "ep", axis=0, tiled=True)
    projected = lax.psum_scatter(
        jnp.dot(all_values, out_proj, preferred_element_type=jnp.float32),
        "kv",
        scatter_dimension=0,
        tiled=True,
    )
    attended = (residual.astype(jnp.float32) + projected).astype(jnp.bfloat16)
    full_width = norm_gain.shape[0]
    attended_wide = attended.astype(jnp.float32)
    squares = lax.psum(jnp.sum(attended_wide * attended_wide, axis=1), "ep")
    inverse = lax.rsqrt(squares / full_width + NORM_EPS)
    col_count = attended.shape[1]
    gain_part = lax.dynamic_slice_in_dim(norm_gain, lax.axis_index("ep") * col_count, col_count, 0)
    normed_part = (attended_wide * inverse[:, None] * gain_part[None, :]).astype(jnp.bfloat16)
    normed = lax.all_gather(normed_part, "ep", axis=1, tiled=True)
    chosen = (route_ids == kv_pos).astype(jnp.float32)
    row_gate = jnp.sum(chosen * route_gates, axis=1)
    w_gate = gate_weight[0]
    w_up = up_weight[0]
    w_down = down_weight[0]
    segment = lax.all_gather(normed, "kv", axis=0, tiled=True)
    gate_act = jnp.dot(segment, w_gate, preferred_element_type=jnp.float32)
    up_act = jnp.dot(segment, w_up, preferred_element_type=jnp.float32)
    hidden = (jax.nn.silu(gate_act) * up_act).astype(jnp.bfloat16)
    expert_terms = jnp.dot(hidden, w_down, preferred_element_type=jnp.float32) * row_gate[:, None]
    by_rows = lax.psum_scatter(
        expert_terms.astype(jnp.bfloat16), "kv", scatter_dimension=0, tiled=True
    )
    combined = lax.psum_scatter(by_rows, "ep", scatter_dimension=1, tiled=True).astype(jnp.float32)
    return (attended, combined.astype(jnp.bfloat16))


def solution(mesh):
    return jax.shard_map(
        on_device,
        mesh=mesh,
        in_specs=(
            P("ep", None, None),
            P("ep", "kv", None),
            P("ep"),
            P("kv", None, None),
            P("kv", "ep"),
            P("kv", "ep"),
            P(),
            P(),
            P(),
            P("kv", None, "ep"),
            P("kv", None, "ep"),
            P("kv", "ep", None),
        ),
        out_specs=(P("kv", "ep"), P("kv", "ep")),
        check_vma=False,
    )
```

profile of v0, /device:TPU:0, one launch (start us, length us, event | category | flops | bytes accessed | tf_op | source)
XLA Modules:
  0.0 372.4 jit_solution(11962655438900803460)
XLA Ops:
  7.2 0.0 copy-start
  7.2 0.9 broadcast_compare_fusion
  8.1 6.4 %fusion.3 = (f32[8,128]{1,0:T(8,128)S(1)}, f32[8,128,1024]{2,1,0:T(8,128)S(1)}) fusion(pred[8,1024]{1,0:T(8,128)(4,1)S(1)} %broadcast_compare_fusion, bf16[8,128,576]{1,2,0:T(8,128)(2,1)} %param.12, bf16[8,1024,576]{1,2,0:T(8,128)(2,1)} %param.13), kind=kOutput, calls=%fused_computation.6 | convolution fusion | flops 1211104256 | bytes 14823424 | tf_op jit(solution)/shard_map/bhc,btc->bht/dot_general | solution.py:31
  14.5 1.9 copy-done.1
  16.4 1.4 fusion.9
  17.8 0.7 copy.28
  18.5 8.0 %all-to-all-start.2 = ((f32[1,8,128]{1,0,2:T(1,128)}), f32[1,8,128]{1,0,2:T(1,128)S(1)}, u32[]{:S(2)}, u32[]{:S(2)}) async-start(f32[1,8,128]{1,0,2:T(1,128)} %copy.28), calls=%async_computation.2 | async-start | bytes 131072 | tf_op jit(solution)/shard_map/all_to_all | solution.py:49
  26.5 0.7 copy.23
  27.2 6.9 %all-to-all-done.2 = f32[1,8,128]{1,0,2:T(1,128)S(1)} async-done(((f32[1,8,128]{1,0,2:T(1,128)}), f32[1,8,128]{1,0,2:T(1,128)S(1)}, u32[]{:S(2)}, u32[]{:S(2)}) %all-to-all-start.2) | async-done | bytes 4128 | tf_op jit(solution)/shard_map/all_to_all | solution.py:49
  34.1 3.5 all-to-all-start
  37.6 7.6 %fusion.18 = f32[1,8,128,512]{3,2,1,0:T(8,128)S(1)} fusion(bf16[8,1024,576]{1,2,0:T(8,128)(2,1)} %param.13, f32[8,128,1024]{2,1,0:T(8,128)} %copy-done.1, f32[8,128]{1,0:T(8,128)S(1)} %get-tuple-element.6, pred[8,1024]{1,0:T(8,128)(4,1)S(1)} %broadcast_compare_fusion), kind=kOutput, calls=%fused_computation.21 | convolution fusion | flops 1078984704 | bytes 14692352 | tf_op jit(solution)/shard_map/bht,btc->bhc/dot_general | solution.py:40
  45.2 2.6 copy.26
  47.8 0.0 all-to-all-done
  47.8 7.3 %all-to-all-start.1 = ((f32[1,8,128,512]{3,1,0,2:T(8,128)}), f32[1,8,128,512]{3,1,0,2:T(8,128)}, u32[]{:S(2)}, u32[]{:S(2)}) async-start(f32[1,8,128,512]{3,1,0,2:T(8,128)} %copy.26), calls=%async_computation.1 | async-start | bytes 4194304 | tf_op jit(solution)/shard_map/all_to_all | solution.py:47
  55.2 0.0 copy-start.7
  55.2 0.0 copy-start.5
  55.2 0.0 copy-start.6
  55.2 0.0 copy-start.4
  55.2 0.0 all-reduce.5.cloned.1.call-start
  55.3 0.1 copy.32
  55.4 0.1 copy.31
  55.5 27.7 %all-to-all-done.1 = f32[1,8,128,512]{3,1,0,2:T(8,128)} async-done(((f32[1,8,128,512]{3,1,0,2:T(8,128)}), f32[1,8,128,512]{3,1,0,2:T(8,128)}, u32[]{:S(2)}, u32[]{:S(2)}) %all-to-all-start.1) | async-done | bytes 2097184 | tf_op jit(solution)/shard_map/all_to_all | solution.py:47
  83.3 2.8 fusion.12
  86.0 0.1 divide_convert_fusion
  86.1 0.3 fusion.29
  86.4 13.3 %all_gather.9 = bf16[64,1024]{1,0:T(8,128)(2,1)S(1)} all-gather(bf16[8,1024]{1,0:T(8,128)(2,1)S(1)} %fusion.29), channel_id=1, replica_groups=mesh['kv'=16,'ep'=8] {'ep'}, dimensions={0}, use_global_device_ids=true | all-gather | bytes 147456 | tf_op jit(solution)/shard_map/all_gather | solution.py:64
  99.7 1.1 fusion.51
  100.8 0.0 all-reduce.5.cloned.1.call-update
  100.8 0.0 all-reduce.7.cloned.1.call-start
  100.9 0.6 dynamic-slice
  102.1 0.8 dynamic_slice.3
  102.9 80.2 %all-reduce.5.cloned.1.call-done = f32[64,896]{1,0:T(8,128)} async-done(((f32[64,896]{1,0:T(8,128)}), f32[64,896]{1,0:T(8,128)}) %all-reduce.5.cloned.1.call-update) | async-done | bytes 229392
  183.1 0.9 fusion.41
  183.9 12.7 %psum.7 = f32[4]{0:T(128)S(1)} all-reduce(f32[4]{0:T(128)S(1)} %get-tuple-element.2), channel_id=1, replica_groups=mesh['kv'=16,'ep'=8] {'ep'}, use_global_device_ids=true, to_apply=%region_7.8 | all-reduce | flops 4 | bytes 32 | tf_op jit(solution)/shard_map/psum | solution.py:74
  196.6 0.1 fusion.43
  196.7 12.8 %all_gather.10 = bf16[4,7168]{1,0:T(4,128)(2,1)S(1)} all-gather(bf16[4,896]{1,0:T(4,128)(2,1)S(1)} %fusion.43), channel_id=1, replica_groups=mesh['kv'=16,'ep'=8] {'ep'}, dimensions={1}, use_global_device_ids=true | all-gather | bytes 64512 | tf_op jit(solution)/shard_map/all_gather | solution.py:79
  209.5 25.2 %all-gather = bf16[16,4,7168]{2,1,0:T(4,128)(2,1)} all-gather(bf16[1,4,7168]{2,1,0:T(4,128)(2,1)S(1)} %bitcast.61), channel_id=1, replica_groups=mesh['kv'=16,'ep'=8] {'kv'}, dimensions={0}, use_global_device_ids=true | all-gather | bytes 974848 | tf_op jit(solution)/shard_map/all_gather | solution.py:85
  234.7 1.7 reshape.54
  236.4 2.8 fusion.7
  239.1 6.4 %fusion.2 = bf16[64,7168]{1,0:T(8,128)(2,1)} fusion(bf16[1,256,7168]{2,1,0:T(8,128)(2,1)} %param.23, f32[64]{0:T(128)S(1)} %select_reduce_fusion, bf16[64,7168]{1,0:T(8,128)(2,1)S(1)} %reshape.54, bf16[1,7168,256]{2,1,0:T(8,128)(2,1)} %param.22, f32[64,256]{1,0:T(8,128)S(1)} %fusion.7), kind=kOutput, calls=%fused_computation.3 | convolution fusion | flops 470777856 | bytes 9240832 | tf_op jit(solution)/shard_map/dot_general | solution.py:89
  245.5 0.0 all-reduce.7.cloned.1.call-update
  245.6 0.0 reduce-scatter.4.cloned.1.call-start
  245.6 83.4 %all-reduce.7.cloned.1.call-done = bf16[64,7168]{1,0:T(8,128)(2,1)} async-done(((bf16[64,7168]{1,0:T(8,128)(2,1)}), bf16[64,7168]{1,0:T(8,128)(2,1)}) %all-reduce.7.cloned.1.call-update) | async-done | bytes 917520
  329.0 0.9 constant_dynamic-slice_fusion
  329.9 1.8 copy.33
  331.7 0.0 reduce-scatter.4.cloned.1.call-update
  331.7 32.5 %reduce-scatter.4.cloned.1.call-done = bf16[896,4]{1,0:T(8,128)(2,1)} async-done(((bf16[7168,4]{1,0:T(8,128)(2,1)}), bf16[896,4]{1,0:T(8,128)(2,1)}) %reduce-scatter.4.cloned.1.call-update) | async-done | bytes 7184
  364.2 1.7 copy.34
  (15 shorter events, 0.1 us)
Async XLA Ops:
  7.2 92.5 %copy-start = (bf16[1024,896]{1,0:T(8,128)(2,1)S(1)}, bf16[1024,896]{1,0:T(8,128)(2,1)}, u32[]{:S(2)}) copy-start(bf16[1024,896]{1,0:T(8,128)(2,1)} %param.16) | copy-start | bytes 5505028
  14.5 1.9 copy-start.1
  18.5 15.6 %all-to-all-start.2 = ((f32[1,8,128]{1,0,2:T(1,128)}), f32[1,8,128]{1,0,2:T(1,128)S(1)}, u32[]{:S(2)}, u32[]{:S(2)}) async-start(f32[1,8,128]{1,0,2:T(1,128)} %copy.28), calls=%async_computation.2 | async-start | bytes 131072 | tf_op jit(solution)/shard_map/all_to_all | solution.py:49
  34.1 13.7 %all-to-all-start = ((f32[1,8,128]{1,0,2:T(1,128)}), f32[1,8,128]{1,0,2:T(1,128)S(1)}, u32[]{:S(2)}, u32[]{:S(2)}) async-start(f32[1,8,128]{1,0,2:T(1,128)} %copy.23), calls=%async_computation | async-start | bytes 131072 | tf_op jit(solution)/shard_map/all_to_all | solution.py:48
  47.8 38.3 %copy-start.2 = (bf16[8,512,128]{2,1,0:T(8,128)(2,1)S(1)}, bf16[8,512,128]{2,1,0:T(8,128)(2,1)}, u32[]{:S(2)}) copy-start(bf16[8,512,128]{2,1,0:T(8,128)(2,1)} %param.15) | copy-start | bytes 3145732
  47.8 35.4 %all-to-all-start.1 = ((f32[1,8,128,512]{3,1,0,2:T(8,128)}), f32[1,8,128,512]{3,1,0,2:T(8,128)}, u32[]{:S(2)}, u32[]{:S(2)}) async-start(f32[1,8,128,512]{3,1,0,2:T(8,128)} %copy.26), calls=%async_computation.1 | async-start | bytes 4194304 | tf_op jit(solution)/shard_map/all_to_all | solution.py:47
  55.2 45.7 %copy-start.7 = (u32[128]{0:T(128)S(1)}, u32[128]{0:T(128)}, u32[]{:S(2)}) copy-start(u32[128]{0:T(128)} %constant.41) | copy-start | bytes 1540
  55.2 47.7 %copy-start.5 = (f32[64,8]{0,1:T(8,128)S(1)}, f32[64,8]{0,1:T(8,128)}, u32[]{:S(2)}) copy-start(f32[64,8]{0,1:T(8,128)} %param.20) | copy-start | bytes 6148
  55.2 47.7 %copy-start.6 = (s32[64,8]{0,1:T(8,128)S(1)}, s32[64,8]{0,1:T(8,128)}, u32[]{:S(2)}) copy-start(s32[64,8]{0,1:T(8,128)} %param.19) | copy-start | bytes 6148
  55.2 127.9 %copy-start.4 = (bf16[4,896]{1,0:T(4,128)(2,1)S(1)}, bf16[4,896]{1,0:T(4,128)(2,1)}, u32[]{:S(2)}) copy-start(bf16[4,896]{1,0:T(4,128)(2,1)} %param.17) | copy-start | bytes 21508
  55.2 127.9 %all-reduce.5.cloned.1.call-start = ((), (), s32[]{:S(2)}) async-start(), calls=%async_computation.5 | async-start | bytes 458752
  100.8 228.2 %all-reduce.7.cloned.1.call-start = ((), (), s32[]{:S(2)}) async-start(), calls=%async_computation.6 | async-start | bytes 1835008
  183.9 61.6 %copy-start.3 = (bf16[4,896]{1,0:T(4,128)(2,1)}, bf16[4,896]{1,0:T(4,128)(2,1)S(1)}, u32[]{:S(2)}) copy-start(bf16[4,896]{1,0:T(4,128)(2,1)S(1)} %get-tuple-element.3) | copy-start | bytes 21508
  245.6 118.6 %reduce-scatter.4.cloned.1.call-start = ((), (), s32[]{:S(2)}) async-start(), calls=%async_computation.4 | async-start | bytes 2064384
Sparse Core Ops, SparseCore 0:
  100.9 82.0 all-reduce.4
  245.7 83.2 all-reduce.6
  331.8 32.2 reduce-scatter.3
where the time goes:
time: 373 us; the launch traced here: 372 us
  waiting for transfers between devices  231 us (62%)
  blocking collectives  63.9 us (17%)
  matrix products  24.6 us (7%)
  starting transfers between devices  18.9 us (5%)
  between operations  14.6 us (4%)
  local copies, waits for them, and re-layouts  13.6 us (4%)
  other arithmetic  6.1 us (2%)
    unnamed x6, waiting for transfers between devices  196 us
    all_to_all x1, waiting for transfers between devices, on_device(): lax.all_to_all(block_out[None], 'kv', split_axis=2, concat_axis=0, tiled=...  27.7 us
    all_gather x1, blocking collectives, on_device(): segment = lax.all_gather(normed, 'kv', axis=0, tiled=True)  25.2 us
    all_gather x1, blocking collectives, on_device(): all_values = lax.all_gather(head_values, 'ep', axis=0, tiled=True)  13.3 us
    all_gather x1, blocking collectives, on_device(): normed = lax.all_gather(normed_part, 'ep', axis=1, tiled=True)  12.8 us
    psum x1, blocking collectives, on_device(): squares = lax.psum(jnp.sum(attended_wide * attended_wide, axis=1), 'ep')  12.7 us
    unnamed x21, local copies, waits for them, and re-layouts  8.57 us
    all_to_all x1, starting transfers between devices, on_device(): lax.all_to_all(block_sum[None], 'kv', split_axis=2, concat_axis=0, tiled=...  7.96 us
  transfers between devices with their start and end apart: 6, of which 5 were waited for; matrix products, arithmetic and copies ran while one was open for 3% of the time, Pallas kernels for 0%

commit v1 on v0

v1 whole, which is shorter than its diff:
```python
import functools

import jax
import jax.numpy as jnp
from jax import lax
from jax.experimental import pallas as pl
from jax.experimental.pallas import tpu as pltpu
from jax.sharding import PartitionSpec as P

SCORE_SCALE = 0.07216878364870323
LOG2_E = 1.4426950408889634
NEG_FILL = -1e30
NORM_EPS = 1e-06
EXTRA = 128
MIB = 1 << 20


def split_three(value):
    high = value.astype(jnp.bfloat16).astype(jnp.float32)
    rest = value - high
    mid = rest.astype(jnp.bfloat16).astype(jnp.float32)
    return high, mid, rest - mid


def attention_kernel(lengths_ref, q_hbm, cache_hbm, out_ref, q_ref, cache_ref, arrived):
    row_count, unused_width, ctx_len = cache_ref.shape
    head_count = q_ref.shape[2]
    groups = out_ref.shape[0]
    lat_width = out_ref.shape[2] - EXTRA
    per_group = head_count // groups

    start = lax.axis_index("kv") * ctx_len

    def fetch(row):
        return (
            pltpu.make_async_copy(q_hbm.at[row], q_ref.at[row], arrived.at[0, row]),
            pltpu.make_async_copy(cache_hbm.at[row], cache_ref.at[row], arrived.at[1, row]),
        )

    for row in range(row_count):
        for copy in fetch(row):
            copy.start()
    lane = lax.broadcasted_iota(jnp.int32, (head_count, EXTRA), 1)
    position = lax.broadcasted_iota(jnp.int32, (head_count, ctx_len), 1)
    for pair in range(0, row_count, 2):
        outs = []
        extras = []
        for row in (pair, pair + 1):
            for copy in fetch(row):
                copy.wait()
            scores = lax.dot_general(
                q_ref[row],
                cache_ref[row],
                (((0,), (0,)), ((), ())),
                preferred_element_type=jnp.float32,
            )
            scores = jnp.where(
                position < lengths_ref[row] - start, scores * (SCORE_SCALE * LOG2_E), NEG_FILL
            )
            top = jnp.max(scores, axis=1, keepdims=True)
            terms = jnp.exp2(scores - top)
            total = jnp.sum(terms, axis=1, keepdims=True)
            out = lax.dot_general(
                terms.astype(jnp.bfloat16),
                cache_ref[row, :lat_width, :],
                (((1,), (1,)), ((), ())),
                preferred_element_type=jnp.float32,
            )
            extra = jnp.zeros((head_count, EXTRA), jnp.float32)
            for at, piece in enumerate(split_three(top) + split_three(total)):
                extra = jnp.where(lane == at, piece, extra)
            outs.append(out.reshape(groups, per_group, lat_width))
            extras.append(extra.reshape(groups, per_group, EXTRA))
        spot = slice(pair * per_group, (pair + 2) * per_group)
        out_ref[:, spot, :lat_width] = jnp.concatenate(outs, axis=1).astype(jnp.bfloat16)
        out_ref[:, spot, lat_width:] = jnp.concatenate(extras, axis=1).astype(jnp.bfloat16)


def attend_block(lengths, queries, latent_cache, groups, lat_width):
    row_count, width, ctx_len = latent_cache.shape
    head_count = queries.shape[2]
    pairs = row_count * (head_count // groups)
    return pl.pallas_call(
        attention_kernel,
        in_specs=[
            pl.BlockSpec(memory_space=pltpu.SMEM),
            pl.BlockSpec(memory_space=pltpu.HBM),
            pl.BlockSpec(memory_space=pltpu.HBM),
        ],
        out_specs=pl.BlockSpec(memory_space=pltpu.VMEM),
        out_shape=jax.ShapeDtypeStruct((groups, pairs, lat_width + EXTRA), jnp.bfloat16),
        scratch_shapes=[
            pltpu.VMEM((row_count, width, head_count), jnp.bfloat16),
            pltpu.VMEM((row_count, width, ctx_len), jnp.bfloat16),
            pltpu.SemaphoreType.DMA((2, row_count)),
        ],
        compiler_params=pltpu.CompilerParams(vmem_limit_bytes=54 * MIB),
        cost_estimate=pl.CostEstimate(
            flops=2 * row_count * head_count * ctx_len * (width + lat_width),
            bytes_accessed=2 * latent_cache.size + 2 * queries.size,
            transcendentals=row_count * head_count * ctx_len,
        ),
        name="attend_block",
    )(lengths, queries, latent_cache)


def merge_kernel(parts_ref, value_ref, out_ref, merged_ref):
    block_count, pairs, wide = parts_ref.shape
    heads, lat_width, value_width = value_ref.shape
    rows = pairs // heads
    extra = parts_ref[:, :, lat_width:].astype(jnp.float32)
    top = extra[:, :, 0:1] + extra[:, :, 1:2] + extra[:, :, 2:3]
    total = extra[:, :, 3:4] + extra[:, :, 4:5] + extra[:, :, 5:6]
    factor = jnp.exp2(top - jnp.max(top, axis=0, keepdims=True))
    denominator = jnp.sum(factor * total, axis=0)
    merged = jnp.zeros((pairs, lat_width), jnp.float32)
    for k in range(block_count):
        merged = merged + factor[k] * parts_ref[k, :, :lat_width].astype(jnp.float32)
    merged = merged / denominator
    tiles = merged_ref.shape[0]
    for t in range(tiles):
        merged_ref[t] = merged[:, t * EXTRA : (t + 1) * EXTRA]
    copies = out_ref.shape[0] // rows
    for h in range(heads):
        attention = jnp.concatenate(
            [merged_ref[t, pl.ds(h, rows, stride=heads), :] for t in range(tiles)], axis=1
        ).astype(jnp.bfloat16)
        value = jnp.dot(attention, value_ref[h], preferred_element_type=jnp.float32)
        out_ref[:, h * value_width : (h + 1) * value_width] = jnp.concatenate(
            [value] * copies, axis=0
        ).astype(jnp.bfloat16)


def merge_blocks(parts, value_up, copies):
    heads, lat_width, value_width = value_up.shape
    pairs = parts.shape[1]
    return pl.pallas_call(
        merge_kernel,
        out_shape=jax.ShapeDtypeStruct(
            (copies * (pairs // heads), heads * value_width), jnp.bfloat16
        ),
        scratch_shapes=[pltpu.VMEM((lat_width // EXTRA, pairs, EXTRA), jnp.float32)],
        compiler_params=pltpu.CompilerParams(vmem_limit_bytes=32 * MIB),
        name="merge_blocks",
    )(parts, value_up)


def residual_kernel(parts_ref, residual_ref, attended_ref, spread_ref):
    total = residual_ref[...].astype(jnp.float32)
    for k in range(parts_ref.shape[0]):
        total = total + parts_ref[k].astype(jnp.float32)
    attended = total.astype(jnp.bfloat16)
    attended_ref[...] = attended
    for i in range(spread_ref.shape[0]):
        spread_ref[i] = attended


def add_residual(parts, residual, copies):
    return pl.pallas_call(
        residual_kernel,
        out_shape=(
            jax.ShapeDtypeStruct(residual.shape, jnp.bfloat16),
            jax.ShapeDtypeStruct((copies,) + residual.shape, jnp.bfloat16),
        ),
        compiler_params=pltpu.CompilerParams(vmem_limit_bytes=8 * MIB),
        cost_estimate=pl.CostEstimate(
            flops=parts.size, bytes_accessed=2 * (copies * residual.size), transcendentals=0
        ),
        name="add_residual",
    )(parts, residual)


def expert_kernel(
    mine_ref,
    other_ref,
    gain_ref,
    ids_ref,
    gates_ref,
    w_gate_hbm,
    w_up_hbm,
    w_down_hbm,
    keep_ref,
    give_ref,
    normed_ref,
    w_gate_ref,
    w_up_ref,
    w_down_ref,
    arrived,
):
    chips, row_count, col_count = mine_ref.shape
    full_width = normed_ref.shape[1]
    part = full_width // chips

    def span(y):
        return slice(y * part, (y + 1) * part)

    def fetch_in(y):
        at = span(y)
        return (
            pltpu.make_async_copy(w_gate_hbm.at[at], w_gate_ref.at[at], arrived.at[0, y]),
            pltpu.make_async_copy(w_up_hbm.at[at], w_up_ref.at[at], arrived.at[1, y]),
        )

    def fetch_out(y):
        at = span(y)
        return pltpu.make_async_copy(
            w_down_hbm.at[:, at], w_down_ref.at[:, at], arrived.at[2, y]
        )

    for y in range(chips):
        for copy in fetch_in(y):
            copy.start()
    for y in range(chips):
        fetch_out(y).start()

    expert = lax.axis_index("kv")
    first = lax.rem(lax.axis_index("ep"), 2) == 0
    squares = jnp.zeros((row_count, col_count), jnp.float32)
    for y in range(chips):
        for piece in (mine_ref[y], other_ref[y]):
            wide = piece.astype(jnp.float32)
            squares = squares + wide * wide
    inverse = lax.rsqrt(jnp.sum(squares, axis=1, keepdims=True) / full_width + NORM_EPS)
    chosen = jnp.where(ids_ref[...] == expert, gates_ref[...], 0.0)
    in_lanes = jnp.sum(chosen, axis=0, keepdims=True)
    square = (row_count, row_count)
    same = lax.broadcasted_iota(jnp.int32, square, 0) == lax.broadcasted_iota(
        jnp.int32, square, 1
    )
    row_gate = jnp.sum(jnp.where(same, in_lanes, 0.0), axis=1, keepdims=True)
    gate_act = jnp.zeros((row_count, w_gate_ref.shape[1]), jnp.float32)
    up_act = gate_act
    for y in range(chips):
        mine = mine_ref[y].astype(jnp.float32)
        other = other_ref[y].astype(jnp.float32)
        for c, piece in enumerate(
            (jnp.where(first, mine, other), jnp.where(first, other, mine))
        ):
            cols = slice((2 * y + c) * col_count, (2 * y + c + 1) * col_count)
            normed_ref[:, cols] = (piece * inverse * gain_ref[:, cols]).astype(jnp.bfloat16)
        for copy in fetch_in(y):
            copy.wait()
        normed = normed_ref[:, span(y)]
        gate_act = gate_act + jnp.dot(
            normed, w_gate_ref[span(y)], preferred_element_type=jnp.float32
        )
        up_act = up_act + jnp.dot(
            normed, w_up_ref[span(y)], preferred_element_type=jnp.float32
        )
    hidden = (gate_act / (1.0 + jnp.exp(-gate_act)) * up_act).astype(jnp.bfloat16)
    for y in range(chips):
        fetch_out(y).wait()
        both = [
            jnp.dot(
                hidden,
                w_down_ref[:, (2 * y + c) * col_count : (2 * y + c + 1) * col_count],
                preferred_element_type=jnp.float32,
            )
            * row_gate
            for c in range(2)
        ]
        keep_ref[y] = jnp.where(first, both[0], both[1]).astype(jnp.bfloat16)
        give_ref[y] = jnp.where(first, both[1], both[0]).astype(jnp.bfloat16)


def run_expert(mine, other, gain, ids, gates, w_gate, w_up, w_down):
    chips, row_count, unused_cols = mine.shape
    full_width, hidden_width = w_gate.shape
    vmem = pl.BlockSpec(memory_space=pltpu.VMEM)
    hbm = pl.BlockSpec(memory_space=pltpu.HBM)
    half = jax.ShapeDtypeStruct(mine.shape, jnp.bfloat16)
    return pl.pallas_call(
        expert_kernel,
        in_specs=[vmem] * 5 + [hbm] * 3,
        out_specs=(vmem, vmem),
        out_shape=(half, half),
        scratch_shapes=[
            pltpu.VMEM((row_count, full_width), jnp.bfloat16),
            pltpu.VMEM(w_gate.shape, jnp.bfloat16),
            pltpu.VMEM(w_up.shape, jnp.bfloat16),
            pltpu.VMEM(w_down.shape, jnp.bfloat16),
            pltpu.SemaphoreType.DMA((3, chips)),
        ],
        compiler_params=pltpu.CompilerParams(vmem_limit_bytes=54 * MIB),
        cost_estimate=pl.CostEstimate(
            flops=6 * row_count * full_width * hidden_width,
            bytes_accessed=6 * full_width * hidden_width,
            transcendentals=row_count * hidden_width,
        ),
        name="run_expert",
    )(mine, other, gain, ids, gates, w_gate, w_up, w_down)


def pair_kernel(keep_ref, given_ref, out_ref):
    chips, row_count, unused_cols = keep_ref.shape
    own_rows = out_ref.shape[1]
    for y in range(chips):
        both = keep_ref[y].astype(jnp.float32) + given_ref[y].astype(jnp.float32)
        for k in range(row_count // own_rows):
            out_ref[y * (row_count // own_rows) + k] = both[
                k * own_rows : (k + 1) * own_rows
            ].astype(jnp.bfloat16)


def add_pair(keep, given, own_rows):
    chips, row_count, col_count = keep.shape
    return pl.pallas_call(
        pair_kernel,
        out_shape=jax.ShapeDtypeStruct(
            (chips * row_count // own_rows, own_rows, col_count), jnp.bfloat16
        ),
        compiler_params=pltpu.CompilerParams(vmem_limit_bytes=8 * MIB),
        cost_estimate=pl.CostEstimate(
            flops=keep.size, bytes_accessed=6 * keep.size, transcendentals=0
        ),
        name="add_pair",
    )(keep, given)


def total_kernel(parts_ref, out_ref):
    total = parts_ref[0].astype(jnp.float32)
    for k in range(1, parts_ref.shape[0]):
        total = total + parts_ref[k].astype(jnp.float32)
    out_ref[...] = total.astype(jnp.bfloat16)


def add_total(parts):
    return pl.pallas_call(
        total_kernel,
        out_shape=jax.ShapeDtypeStruct(parts.shape[1:], jnp.bfloat16),
        compiler_params=pltpu.CompilerParams(vmem_limit_bytes=8 * MIB),
        name="add_total",
    )(parts)


def on_device(
    queries,
    latent_cache,
    lengths,
    value_up,
    out_proj,
    residual,
    norm_gain,
    route_ids,
    route_gates,
    gate_weight,
    up_weight,
    down_weight,
):
    kv_count = lax.axis_size("kv")
    ep_count = lax.axis_size("ep")
    chips = ep_count // 2
    both = ("kv", "ep")
    same_core = [
        [kv * ep_count + y * 2 + c for y in range(chips) for kv in range(kv_count)]
        for c in range(2)
    ]
    other_core = [(i, i ^ 1) for i in range(ep_count)]
    lat_width = value_up.shape[1]

    parts = attend_block(
        lengths,
        jnp.swapaxes(queries, 1, 2),
        jnp.swapaxes(latent_cache, 1, 2),
        kv_count,
        lat_width,
    )
    parts = lax.all_to_all(parts, "kv", split_axis=0, concat_axis=0, tiled=True)
    head_values = merge_blocks(parts, value_up, ep_count)
    all_values = lax.all_to_all(head_values, "ep", split_axis=0, concat_axis=0, tiled=True)
    row_count = all_values.shape[0]
    col_count = out_proj.shape[1]
    own_rows = row_count // kv_count
    projected = jnp.dot(all_values, out_proj, preferred_element_type=jnp.float32)
    projected = projected.astype(jnp.bfloat16).reshape(kv_count, own_rows, col_count)
    projected = lax.all_to_all(projected, "kv", split_axis=0, concat_axis=0, tiled=True)
    attended, spread = add_residual(projected, residual, kv_count * chips)

    mine = lax.all_to_all(
        spread, both, split_axis=0, concat_axis=0, tiled=True, axis_index_groups=same_core
    ).reshape(chips, row_count, col_count)
    other = lax.ppermute(mine, "ep", other_core)
    keep, give = run_expert(
        mine,
        other,
        norm_gain[None],
        route_ids.T,
        route_gates.T,
        gate_weight[0],
        up_weight[0],
        down_weight[0],
    )
    given = lax.ppermute(give, "ep", other_core)
    summed = add_pair(keep, given, own_rows)
    arrived = lax.all_to_all(
        summed, both, split_axis=0, concat_axis=0, tiled=True, axis_index_groups=same_core
    )
    return (attended, add_total(arrived))


def solution(mesh):
    return jax.shard_map(
        on_device,
        mesh=mesh,
        in_specs=(
            P("ep", None, None),
            P("ep", "kv", None),
            P("ep"),
            P("kv", None, None),
            P("kv", "ep"),
            P("kv", "ep"),
            P(),
            P(),
            P(),
            P("kv", None, "ep"),
            P("kv", None, "ep"),
            P("kv", "ep", None),
        ),
        out_specs=(P("kv", "ep"), P("kv", "ep")),
        check_vma=False,
    )
```

time: 373 us -> 111 us (0.30)
  waiting for transfers between devices: 231 us -> 3.69 us
  matrix products: 24.6 us -> 0.43 us
  blocking collectives: 63.9 us -> 83.7 us
  Pallas kernels: 0 us -> 19.4 us
  starting transfers between devices: 18.9 us -> 0.3 us
  between operations: 14.6 us -> 0.72 us
  local copies, waits for them, and re-layouts: 13.6 us -> 1.95 us
  other arithmetic: 6.1 us -> 0 us
    unnamed x6 -> x0, waiting for transfers between devices: 196 us -> none
    all_to_all x0 -> x5, blocking collectives: none -> 83.7 us  [the longest x1 27.8 us: on_device(): parts = lax.all_to_all(parts, 'kv', split_axis=0, concat_axis=0, tiled=True)]
    all_gather x3 -> x0, blocking collectives: 51.2 us -> none  [the longest x1 25.2 us: on_device(): segment = lax.all_gather(normed, 'kv', axis=0, tiled=True)]
    all_to_all x3 -> x0, waiting for transfers between devices: 34.7 us -> none  [the longest x1 27.7 us: on_device(): lax.all_to_all(block_out[None], 'kv', split_axis=2, concat_axis=0, tiled=...]
    dot_general x5 -> x0, matrix products: 23.5 us -> none  [the longest x1 7.59 us: on_device(): jnp.einsum('bht,btc->bhc', exp_terms.astype(jnp.bfloat16), latent_cache[:...]
    pallas_call x0 -> x6, Pallas kernels: none -> 19.4 us  [the longest x1 10.2 us: attend_block(): pl.pallas_call(attention_kernel, in_specs=[pl.BlockSpec(memory_space=pltp...]
    all_to_all x3 -> x0, starting transfers between devices: 18.8 us -> none  [the longest x1 7.96 us: on_device(): lax.all_to_all(block_sum[None], 'kv', split_axis=2, concat_axis=0, tiled=...]
    psum x1 -> x0, blocking collectives: 12.7 us -> none  [on_device(): squares = lax.psum(jnp.sum(attended_wide * attended_wide, axis=1), 'ep')]
  transfers between devices with their start and end apart: 6 -> 2, of which waited for: 5 -> 2; matrix products, arithmetic and copies ran while one was open for 3% -> 0% of each run, Pallas kernels for 0% -> 0%
where the time goes in v1:
time: 111 us; the launch traced here: 110 us
  blocking collectives  83.7 us (75%)
  Pallas kernels  19.4 us (17%)
  waiting for transfers between devices  3.69 us (3%)
  local copies, waits for them, and re-layouts  1.95 us (2%)
    all_to_all x1, blocking collectives, on_device(): parts = lax.all_to_all(parts, 'kv', split_axis=0, concat_axis=0, tiled=True)  27.8 us
    all_to_all x1, blocking collectives, on_device(): lax.all_to_all(summed, both, split_axis=0, concat_axis=0, tiled=True, axi...  17.5 us
    all_to_all x1, blocking collectives, on_device(): lax.all_to_all(spread, both, split_axis=0, concat_axis=0, tiled=True, axi...  16.4 us
    all_to_all x1, blocking collectives, on_device(): lax.all_to_all(projected, 'kv', split_axis=0, concat_axis=0, tiled=True)  11.4 us
    all_to_all x1, blocking collectives, on_device(): lax.all_to_all(head_values, 'ep', split_axis=0, concat_axis=0, tiled=True)  10.5 us
    pallas_call x1, Pallas kernels, attend_block(): pl.pallas_call(attention_kernel, in_specs=[pl.BlockSpec(memory_space=pltp...  10.2 us
    pallas_call x1, Pallas kernels, run_expert(): pl.pallas_call(expert_kernel, in_specs=[vmem] * 5 + [hbm] * 3, out_specs=...  6.93 us
  transfers between devices with their start and end apart: 2, of which 2 were waited for; matrix products, arithmetic and copies ran while one was open for 0% of the time, Pallas kernels for 0%

profile of v1, /device:TPU:0, one launch (start us, length us, event | category | flops | bytes accessed | tf_op | source)
XLA Modules:
  0.0 110.2 jit_solution(12793742800308079830)
XLA Ops:
  0.6 0.0 copy-start
  0.6 10.2 %attend_block.1 = bf16[16,64,640]{2,1,0:T(8,128)(2,1)} custom-call(s32[8]{0:T(128)} %lengths_ref.1, bf16[8,576,128]{2,1,0:T(8,128)(2,1)} %bitcast.18, bf16[8,576,1024]{2,1,0:T(8,128)(2,1)} %bitcast.14), custom_call_target="tpu_custom_call" | custom-call | flops 2281701376 | bytes 10616832 | tf_op jit(solution)/shard_map/attend_block/pallas_call | solution.py:83
  10.9 0.0 copy-start.1
  10.9 27.8 %all_to_all.32.parts_ref = bf16[16,64,640]{2,1,0:T(8,128)(2,1)S(1)} all-to-all(bf16[16,64,640]{2,1,0:T(8,128)(2,1)} %attend_block.1), channel_id=1, replica_groups=mesh['kv'=16,'ep'=8] {'kv'}, dimensions={0} | all-to-all | bytes 2621440 | tf_op jit(solution)/shard_map/all_to_all | solution.py:368
  38.8 0.0 copy-done.1
  38.8 0.8 merge_blocks.1
  39.6 0.0 copy-start.3
  39.6 10.5 %all_to_all.33 = bf16[8,8,1024]{2,1,0:T(8,128)(2,1)S(1)} all-to-all(bf16[8,8,1024]{2,1,0:T(8,128)(2,1)S(1)} %bitcast.13), channel_id=1, replica_groups=mesh['kv'=16,'ep'=8] {'ep'}, dimensions={0} | all-to-all | bytes 262144 | tf_op jit(solution)/shard_map/all_to_all | solution.py:370
  50.1 0.0 copy-done
  50.1 0.4 convolution_convert_fusion
  50.6 11.4 %all_to_all.34.parts_ref = bf16[16,4,896]{2,1,0:T(4,128)(2,1)S(1)} all-to-all(bf16[16,4,896]{2,1,0:T(4,128)(2,1)S(1)} %reshape.12), channel_id=1, replica_groups=mesh['kv'=16,'ep'=8] {'kv'}, dimensions={0} | all-to-all | bytes 229376 | tf_op jit(solution)/shard_map/all_to_all | solution.py:376
  62.0 0.0 copy-done.3
  62.0 0.6 add_residual.1
  62.6 16.4 %all_to_all.35 = bf16[64,4,896]{2,1,0:T(4,128)(2,1)S(1)} all-to-all(bf16[64,4,896]{2,1,0:T(4,128)(2,1)S(1)} %get-tuple-element.7), channel_id=1, replica_groups={{0,8,16,24,32,40,48,56,64,72,80,88,96,104,112,120,2,10,18,26,34,42,50,5..., dimensions={0} | all-to-all | bytes 917504 | tf_op jit(solution)/shard_map/all_to_all | solution.py:379
  79.0 0.1 reshape.13.mine_ref
  79.1 0.0 copy-start.4
  79.1 0.1 collective-permute-start
  79.2 1.8 %collective-permute-done.other_ref = bf16[4,64,896]{2,1,0:T(8,128)(2,1)S(1)} collective-permute-done((bf16[4,64,896]{2,1,0:T(8,128)(2,1)S(1)}, bf16[4,64,896]{2,1,0:T(8,128)(2,1)S(1)}, u32[]{:S(2)}, u32[]{:S(2)}) %collective-permute-start) | collective-permute-done | bytes 458784 | tf_op jit(solution)/shard_map/ppermute | solution.py:382
  81.0 0.0 copy-start.5
  81.0 0.0 copy-done.4
  81.0 0.8 copy-done.5
  81.8 6.9 %run_expert.1 = (bf16[4,64,896]{2,1,0:T(8,128)(2,1)}, bf16[4,64,896]{2,1,0:T(8,128)(2,1)}) custom-call(bf16[4,64,896]{2,1,0:T(8,128)(2,1)} %copy-done.4, bf16[4,64,896]{2,1,0:T(8,128)(2,1)} %copy-done.5, f32[1,7168]{1,0:T(1,128)} %bitcast.19, s32[8,64]{1,0:T(8,128)} %bitcast.20, f32[8,64]{1,0:T(8,128)} %bitcast.21, bf16[7168,256]{1,0:T(8,128)(2,1)} %bitcast.15, ...), custom_call_target="tpu_custom_call" | custom-call | flops 704643072 | bytes 11010048 | tf_op jit(solution)/shard_map/run_expert/pallas_call | solution.py:272
  88.7 0.2 collective-permute-start.1
  88.9 1.9 %collective-permute-done.1.given_ref = bf16[4,64,896]{2,1,0:T(8,128)(2,1)S(1)} collective-permute-done((bf16[4,64,896]{2,1,0:T(8,128)(2,1)}, bf16[4,64,896]{2,1,0:T(8,128)(2,1)S(1)}, u32[]{:S(2)}, u32[]{:S(2)}) %collective-permute-start.1) | collective-permute-done | bytes 458784 | tf_op jit(solution)/shard_map/ppermute | solution.py:393
  90.8 0.0 copy-start.2
  90.8 1.0 copy-done.2
  91.8 0.1 add_pair.1
  92.0 17.5 %all_to_all.36.parts_ref = bf16[64,4,896]{2,1,0:T(4,128)(2,1)S(1)} all-to-all(bf16[64,4,896]{2,1,0:T(4,128)(2,1)S(1)} %add_pair.1), channel_id=1, replica_groups={{0,8,16,24,32,40,48,56,64,72,80,88,96,104,112,120,2,10,18,26,34,42,50,5..., dimensions={0} | all-to-all | bytes 917504 | tf_op jit(solution)/shard_map/all_to_all | solution.py:395
  109.5 0.7 add_total.1
  (1 shorter events, 0.0 us)
Async XLA Ops:
  0.6 49.5 %copy-start = (bf16[1024,896]{1,0:T(8,128)(2,1)S(1)}, bf16[1024,896]{1,0:T(8,128)(2,1)}, u32[]{:S(2)}) copy-start(bf16[1024,896]{1,0:T(8,128)(2,1)} %param.16) | copy-start | bytes 5505028
  10.9 27.9 %copy-start.1 = (bf16[8,512,128]{2,1,0:T(8,128)(2,1)S(1)}, bf16[8,512,128]{2,1,0:T(8,128)(2,1)}, u32[]{:S(2)}) copy-start(bf16[8,512,128]{2,1,0:T(8,128)(2,1)} %value_ref.1) | copy-start | bytes 3145732
  39.6 22.4 %copy-start.3 = (bf16[4,896]{1,0:T(4,128)(2,1)S(1)}, bf16[4,896]{1,0:T(4,128)(2,1)}, u32[]{:S(2)}) copy-start(bf16[4,896]{1,0:T(4,128)(2,1)} %residual_ref.1) | copy-start | bytes 21508
  79.1 1.9 %copy-start.4 = (bf16[4,64,896]{2,1,0:T(8,128)(2,1)}, bf16[4,64,896]{2,1,0:T(8,128)(2,1)S(1)}, u32[]{:S(2)}) copy-start(bf16[4,64,896]{2,1,0:T(8,128)(2,1)S(1)} %reshape.13.mine_ref) | copy-start | bytes 1376260
  79.1 1.9 %collective-permute-start = (bf16[4,64,896]{2,1,0:T(8,128)(2,1)S(1)}, bf16[4,64,896]{2,1,0:T(8,128)(2,1)S(1)}, u32[]{:S(2)}, u32[]{:S(2)}) collective-permute-start(bf16[4,64,896]{2,1,0:T(8,128)(2,1)S(1)} %reshape.13.mine_ref), channel_id=1, source_target_pairs={{0,1},{1,0},{2,3},{3,2},{4,5},{5,4},{6,7},{7,6},{8,9},{9,8},{10,11... | collective-permute-start | bytes 1376264 | tf_op jit(solution)/shard_map/ppermute | solution.py:382
  81.0 0.8 copy-start.5
  88.7 2.1 %collective-permute-start.1 = (bf16[4,64,896]{2,1,0:T(8,128)(2,1)}, bf16[4,64,896]{2,1,0:T(8,128)(2,1)S(1)}, u32[]{:S(2)}, u32[]{:S(2)}) collective-permute-start(bf16[4,64,896]{2,1,0:T(8,128)(2,1)} %get-tuple-element.9), channel_id=1, source_target_pairs={{0,1},{1,0},{2,3},{3,2},{4,5},{5,4},{6,7},{7,6},{8,9},{9,8},{10,11... | collective-permute-start | bytes 1376264 | tf_op jit(solution)/shard_map/ppermute | solution.py:393
  90.8 1.0 copy-start.2

commit v2 on v1

v2 whole, which is shorter than its diff:
```python
import functools

import jax
import jax.numpy as jnp
from jax import lax
from jax.experimental import pallas as pl
from jax.experimental.pallas import tpu as pltpu
from jax.sharding import PartitionSpec as P

SCORE_SCALE = 0.07216878364870323
LOG2_E = 1.4426950408889634
NEG_FILL = -1e30
NORM_EPS = 1e-06
LANES = 128
MIB = 1 << 20


def in_hbm(array):
    return pltpu.with_memory_space_constraint(array, pltpu.HBM)


def split_three(value):
    high = value.astype(jnp.bfloat16).astype(jnp.float32)
    rest = value - high
    mid = rest.astype(jnp.bfloat16).astype(jnp.float32)
    return high, mid, rest - mid


def attention_kernel(lengths_ref, q_hbm, cache_hbm, *refs):
    weight_count = (len(refs) - 4) // 2
    weights_hbm = refs[:weight_count]
    out_ref = refs[weight_count]
    weights_ref = refs[weight_count + 1 : -3]
    q_ref, cache_ref, arrived = refs[-3:]
    row_count, unused_width, ctx_len = cache_ref.shape
    head_count = q_ref.shape[2]
    groups = out_ref.shape[0]
    lat_width = out_ref.shape[2]
    per_group = head_count // groups
    start = lax.axis_index("kv") * ctx_len

    def fetch(row):
        return (
            pltpu.make_async_copy(q_hbm.at[row], q_ref.at[row], arrived.at[0, row]),
            pltpu.make_async_copy(cache_hbm.at[row], cache_ref.at[row], arrived.at[1, row]),
        )

    extra_copies = [
        pltpu.make_async_copy(weights_hbm[i], weights_ref[i], arrived.at[2, i])
        for i in range(weight_count)
    ]
    for row in range(row_count):
        for copy in fetch(row):
            copy.start()
    for copy in extra_copies:
        copy.start()
    position = lax.broadcasted_iota(jnp.int32, (head_count, ctx_len), 1)
    square = (head_count, head_count)
    same = lax.broadcasted_iota(jnp.int32, square, 0) == lax.broadcasted_iota(
        jnp.int32, square, 1
    )
    line = lax.broadcasted_iota(jnp.int32, (row_count, head_count), 0)
    levels = jnp.zeros((row_count, head_count), jnp.float32)
    for pair in range(0, row_count, 2):
        rows = (pair, pair + 1)
        for row in rows:
            for copy in fetch(row):
                copy.wait()
        scores = [
            lax.dot_general(
                q_ref[row],
                cache_ref[row],
                (((0,), (0,)), ((), ())),
                preferred_element_type=jnp.float32,
            )
            for row in rows
        ]
        scores = [
            jnp.where(position < lengths_ref[row] - start, s * (SCORE_SCALE * LOG2_E), NEG_FILL)
            for row, s in zip(rows, scores)
        ]
        tops = [jnp.max(s, axis=1, keepdims=True) for s in scores]
        terms = [jnp.exp2(s - top) for s, top in zip(scores, tops)]
        totals = [jnp.sum(t, axis=1, keepdims=True) for t in terms]
        outs = [
            lax.dot_general(
                t.astype(jnp.bfloat16),
                cache_ref[row, :lat_width, :],
                (((1,), (1,)), ((), ())),
                preferred_element_type=jnp.float32,
            )
            for row, t in zip(rows, terms)
        ]
        outs = [
            (o * (1.0 / total)).reshape(groups, per_group, lat_width)
            for o, total in zip(outs, totals)
        ]
        spot = slice(pair * per_group, (pair + 2) * per_group)
        out_ref[:, spot, :] = jnp.concatenate(outs, axis=1).astype(jnp.bfloat16)
        for row, top, total in zip(rows, tops, totals):
            level = jnp.sum(
                jnp.where(same, top + jnp.log2(total), 0.0), axis=0, keepdims=True
            )
            levels = jnp.where(line == row, level, levels)
    blank = jnp.zeros((row_count, lat_width - 3 * head_count), jnp.float32)
    stats = jnp.concatenate(split_three(levels) + (blank,), axis=1).astype(jnp.bfloat16)
    for k in range(groups):
        out_ref[k, row_count * per_group :, :] = stats
    for copy in extra_copies:
        copy.wait()


def attend_block(lengths, queries, latent_cache, groups, lat_width, weights):
    row_count, width, ctx_len = latent_cache.shape
    head_count = queries.shape[2]
    pairs = row_count * (head_count // groups)
    hbm = pl.BlockSpec(memory_space=pltpu.HBM)
    vmem = pl.BlockSpec(memory_space=pltpu.VMEM)
    return pl.pallas_call(
        attention_kernel,
        in_specs=[pl.BlockSpec(memory_space=pltpu.SMEM)] + [hbm] * (2 + len(weights)),
        out_specs=[vmem] * (1 + len(weights)),
        out_shape=[jax.ShapeDtypeStruct((groups, pairs + row_count, lat_width), jnp.bfloat16)]
        + [pltpu.VMEM(w.shape, w.dtype) for w in weights],
        scratch_shapes=[
            pltpu.VMEM((row_count, width, head_count), jnp.bfloat16),
            pltpu.VMEM((row_count, width, ctx_len), jnp.bfloat16),
            pltpu.SemaphoreType.DMA((3, row_count)),
        ],
        compiler_params=pltpu.CompilerParams(vmem_limit_bytes=28 * MIB),
        cost_estimate=pl.CostEstimate(
            flops=2 * row_count * head_count * ctx_len * (width + lat_width),
            bytes_accessed=2 * latent_cache.size + 2 * queries.size,
            transcendentals=row_count * head_count * ctx_len,
        ),
        name="attend_block",
    )(in_hbm(lengths), in_hbm(queries), in_hbm(latent_cache), *(in_hbm(w) for w in weights))


def merge_kernel(parts_ref, value_ref, *refs):
    out_ref, merged_ref = refs[-2:]
    block_count = parts_ref.shape[0]
    heads, lat_width, value_width = value_ref.shape
    rows = parts_ref.shape[1] // (heads + 1)
    pairs = rows * heads
    lanes = heads * block_count
    stats = parts_ref[:, pairs:, :].astype(jnp.float32)
    levels = (
        stats[:, :, :lanes] + stats[:, :, lanes : 2 * lanes] + stats[:, :, 2 * lanes : 3 * lanes]
    )
    factor = jnp.exp2(levels - jnp.max(levels, axis=0, keepdims=True))
    factor = factor / jnp.sum(factor, axis=0, keepdims=True)
    shape = (rows, heads, lanes)
    own = lax.broadcasted_iota(jnp.int32, shape, 2) == lax.broadcasted_iota(
        jnp.int32, shape, 1
    ) + heads * lax.axis_index("kv")
    merged = jnp.zeros((pairs, lat_width), jnp.float32)
    for k in range(block_count):
        column = jnp.sum(jnp.where(own, factor[k][:, None, :], 0.0), axis=2, keepdims=True)
        merged = merged + column.reshape(pairs, 1) * parts_ref[k, :pairs, :].astype(jnp.float32)
    tiles = merged_ref.shape[0]
    for t in range(tiles):
        merged_ref[t] = merged[:, t * LANES : (t + 1) * LANES]
    copies = out_ref.shape[0] // rows
    for h in range(heads):
        attention = jnp.concatenate(
            [merged_ref[t, pl.ds(h, rows, stride=heads), :] for t in range(tiles)], axis=1
        ).astype(jnp.bfloat16)
        value = jnp.dot(attention, value_ref[h], preferred_element_type=jnp.float32)
        out_ref[:, h * value_width : (h + 1) * value_width] = jnp.concatenate(
            [value] * copies, axis=0
        ).astype(jnp.bfloat16)


def merge_blocks(parts, value_up, copies, held):
    heads, lat_width, value_width = value_up.shape
    pairs = parts.shape[1] // (heads + 1) * heads
    return pl.pallas_call(
        merge_kernel,
        out_shape=jax.ShapeDtypeStruct(
            (copies * (pairs // heads), heads * value_width), jnp.bfloat16
        ),
        scratch_shapes=[pltpu.VMEM((lat_width // LANES, pairs, LANES), jnp.float32)],
        compiler_params=pltpu.CompilerParams(vmem_limit_bytes=12 * MIB),
        name="merge_blocks",
    )(parts, value_up, *held)


def project_kernel(values_ref, proj_ref, *refs):
    out_ref = refs[-1]
    own_rows = out_ref.shape[1]
    projected = jnp.dot(values_ref[...], proj_ref[...], preferred_element_type=jnp.float32)
    for k in range(out_ref.shape[0]):
        out_ref[k] = projected[k * own_rows : (k + 1) * own_rows].astype(jnp.bfloat16)


def project(values, proj, groups, held):
    rows = values.shape[0]
    cols = proj.shape[1]
    return pl.pallas_call(
        project_kernel,
        out_shape=jax.ShapeDtypeStruct((groups, rows // groups, cols), jnp.bfloat16),
        compiler_params=pltpu.CompilerParams(vmem_limit_bytes=12 * MIB),
        cost_estimate=pl.CostEstimate(
            flops=2 * rows * proj.size, bytes_accessed=2 * proj.size, transcendentals=0
        ),
        name="project",
    )(values, proj, *held)


def residual_kernel(parts_ref, residual_ref, *refs):
    attended_ref, spread_ref = refs[-2:]
    total = residual_ref[...].astype(jnp.float32)
    for k in range(parts_ref.shape[0]):
        total = total + parts_ref[k].astype(jnp.float32)
    attended = total.astype(jnp.bfloat16)
    attended_ref[...] = attended
    for i in range(spread_ref.shape[0]):
        spread_ref[i] = attended


def add_residual(parts, residual, copies, held):
    return pl.pallas_call(
        residual_kernel,
        out_shape=(
            jax.ShapeDtypeStruct(residual.shape, jnp.bfloat16),
            jax.ShapeDtypeStruct((copies,) + residual.shape, jnp.bfloat16),
        ),
        compiler_params=pltpu.CompilerParams(vmem_limit_bytes=8 * MIB),
        cost_estimate=pl.CostEstimate(
            flops=parts.size, bytes_accessed=2 * copies * residual.size, transcendentals=0
        ),
        name="add_residual",
    )(parts, residual, *held)


def expert_kernel(
    mine_ref,
    other_ref,
    gain_ref,
    ids_ref,
    gates_ref,
    w_gate_ref,
    w_up_ref,
    w_down_ref,
    keep_ref,
    give_ref,
    normed_ref,
):
    chips, row_count, col_count = mine_ref.shape
    full_width = normed_ref.shape[1]
    expert = lax.axis_index("kv")
    first = lax.rem(lax.axis_index("ep"), 2) == 0
    squares = jnp.zeros((row_count, col_count), jnp.float32)
    for y in range(chips):
        for piece in (mine_ref[y], other_ref[y]):
            wide = piece.astype(jnp.float32)
            squares = squares + wide * wide
    inverse = lax.rsqrt(jnp.sum(squares, axis=1, keepdims=True) / full_width + NORM_EPS)
    chosen = jnp.where(ids_ref[...] == expert, gates_ref[...], 0.0)
    in_lanes = jnp.sum(chosen, axis=0, keepdims=True)
    square = (row_count, row_count)
    same = lax.broadcasted_iota(jnp.int32, square, 0) == lax.broadcasted_iota(
        jnp.int32, square, 1
    )
    row_gate = jnp.sum(jnp.where(same, in_lanes, 0.0), axis=1, keepdims=True)
    for y in range(chips):
        mine = mine_ref[y].astype(jnp.float32)
        other = other_ref[y].astype(jnp.float32)
        for c, piece in enumerate(
            (jnp.where(first, mine, other), jnp.where(first, other, mine))
        ):
            cols = slice((2 * y + c) * col_count, (2 * y + c + 1) * col_count)
            normed_ref[:, cols] = (piece * inverse * gain_ref[:, cols]).astype(jnp.bfloat16)
    normed = normed_ref[...]
    gate_act = jnp.dot(normed, w_gate_ref[...], preferred_element_type=jnp.float32)
    up_act = jnp.dot(normed, w_up_ref[...], preferred_element_type=jnp.float32)
    hidden = (gate_act / (1.0 + jnp.exp(-gate_act)) * up_act).astype(jnp.bfloat16)
    for y in range(chips):
        both = [
            jnp.dot(
                hidden,
                w_down_ref[:, (2 * y + c) * col_count : (2 * y + c + 1) * col_count],
                preferred_element_type=jnp.float32,
            )
            * row_gate
            for c in range(2)
        ]
        keep_ref[y] = jnp.where(first, both[0], both[1]).astype(jnp.bfloat16)
        give_ref[y] = jnp.where(first, both[1], both[0]).astype(jnp.bfloat16)


def run_expert(mine, other, gain, ids, gates, w_gate, w_up, w_down):
    row_count = mine.shape[1]
    full_width, hidden_width = w_gate.shape
    vmem = pl.BlockSpec(memory_space=pltpu.VMEM)
    half = jax.ShapeDtypeStruct(mine.shape, jnp.bfloat16)
    return pl.pallas_call(
        expert_kernel,
        in_specs=[vmem] * 8,
        out_specs=(vmem, vmem),
        out_shape=(half, half),
        scratch_shapes=[pltpu.VMEM((row_count, full_width), jnp.bfloat16)],
        compiler_params=pltpu.CompilerParams(vmem_limit_bytes=12 * MIB),
        cost_estimate=pl.CostEstimate(
            flops=6 * row_count * full_width * hidden_width,
            bytes_accessed=6 * full_width * hidden_width,
            transcendentals=row_count * hidden_width,
        ),
        name="run_expert",
    )(mine, other, gain, ids, gates, w_gate, w_up, w_down)


def pair_kernel(keep_ref, given_ref, out_ref):
    chips, row_count, unused_cols = keep_ref.shape
    own_rows = out_ref.shape[1]
    for y in range(chips):
        both = keep_ref[y].astype(jnp.float32) + given_ref[y].astype(jnp.float32)
        for k in range(row_count // own_rows):
            out_ref[y * (row_count // own_rows) + k] = both[
                k * own_rows : (k + 1) * own_rows
            ].astype(jnp.bfloat16)


def add_pair(keep, given, own_rows):
    chips, row_count, col_count = keep.shape
    return pl.pallas_call(
        pair_kernel,
        out_shape=jax.ShapeDtypeStruct(
            (chips * row_count // own_rows, own_rows, col_count), jnp.bfloat16
        ),
        compiler_params=pltpu.CompilerParams(vmem_limit_bytes=8 * MIB),
        cost_estimate=pl.CostEstimate(
            flops=keep.size, bytes_accessed=6 * keep.size, transcendentals=0
        ),
        name="add_pair",
    )(keep, given)


def total_kernel(parts_ref, out_ref):
    total = parts_ref[0].astype(jnp.float32)
    for k in range(1, parts_ref.shape[0]):
        total = total + parts_ref[k].astype(jnp.float32)
    out_ref[...] = total.astype(jnp.bfloat16)


def regroup_kernel(parts_ref, *refs):
    out_ref = refs[-1]
    chips = out_ref.shape[0]
    each = parts_ref.shape[0] // chips
    for y in range(chips):
        out_ref[y] = jnp.concatenate(
            [parts_ref[y * each + k].astype(jnp.float32) for k in range(each)], axis=0
        ).astype(jnp.bfloat16)


def regroup(parts, chips, held):
    count, rows, cols = parts.shape
    return pl.pallas_call(
        regroup_kernel,
        out_shape=jax.ShapeDtypeStruct((chips, count // chips * rows, cols), jnp.bfloat16),
        compiler_params=pltpu.CompilerParams(vmem_limit_bytes=8 * MIB),
        name="regroup",
    )(parts, *held)


def add_total(parts):
    return pl.pallas_call(
        total_kernel,
        out_shape=jax.ShapeDtypeStruct(parts.shape[1:], jnp.bfloat16),
        compiler_params=pltpu.CompilerParams(vmem_limit_bytes=8 * MIB),
        name="add_total",
    )(parts)


def on_device(
    queries,
    latent_cache,
    lengths,
    value_up,
    out_proj,
    residual,
    norm_gain,
    route_ids,
    route_gates,
    gate_weight,
    up_weight,
    down_weight,
):
    kv_count = lax.axis_size("kv")
    ep_count = lax.axis_size("ep")
    chips = ep_count // 2
    both = ("kv", "ep")
    same_core = [
        [kv * ep_count + y * 2 + c for y in range(chips) for kv in range(kv_count)]
        for c in range(2)
    ]
    other_core = [(i, i ^ 1) for i in range(ep_count)]
    lat_width = value_up.shape[1]

    parts, *weights = attend_block(
        lengths,
        jnp.swapaxes(queries, 1, 2),
        jnp.swapaxes(latent_cache, 1, 2),
        kv_count,
        lat_width,
        (gate_weight[0], up_weight[0], down_weight[0]),
    )
    parts = lax.all_to_all(parts, "kv", split_axis=0, concat_axis=0, tiled=True)
    head_values = merge_blocks(parts, value_up, ep_count, weights)
    all_values = lax.all_to_all(head_values, "ep", split_axis=0, concat_axis=0, tiled=True)
    own_rows = all_values.shape[0] // kv_count
    projected = project(all_values, out_proj, kv_count, weights)
    projected = lax.all_to_all(projected, "kv", split_axis=0, concat_axis=0, tiled=True)
    attended, spread = add_residual(projected, residual, kv_count * chips, weights)

    mine = lax.all_to_all(
        spread, both, split_axis=0, concat_axis=0, tiled=True, axis_index_groups=same_core
    )
    mine = regroup(mine, chips, weights)
    other = lax.ppermute(mine, "ep", other_core)
    keep, give = run_expert(
        mine,
        other,
        norm_gain[None],
        route_ids.T,
        route_gates.T,
        *weights,
    )
    given = lax.ppermute(give, "ep", other_core)
    summed = add_pair(keep, given, own_rows)
    arrived = lax.all_to_all(
        summed, both, split_axis=0, concat_axis=0, tiled=True, axis_index_groups=same_core
    )
    return (attended, add_total(arrived))


def solution(mesh):
    return jax.shard_map(
        on_device,
        mesh=mesh,
        in_specs=(
            P("ep", None, None),
            P("ep", "kv", None),
            P("ep"),
            P("kv", None, None),
            P("kv", "ep"),
            P("kv", "ep"),
            P(),
            P(),
            P(),
            P("kv", None, "ep"),
            P("kv", None, "ep"),
            P("kv", "ep", None),
        ),
        out_specs=(P("kv", "ep"), P("kv", "ep")),
        check_vma=False,
    )
```

time: 111 us -> 99.8 us (0.90)
  Pallas kernels: 19.4 us -> 13.2 us
  local copies, waits for them, and re-layouts: 1.95 us -> 0.02 us
  blocking collectives: 83.7 us -> 81.8 us
    pallas_call x1 -> x3, Pallas kernels: 6.93 us -> 2.82 us  [the longest x1 2.28 us: run_expert(): pl.pallas_call(expert_kernel, in_specs=[vmem] * 8, out_specs=(vmem, vmem)...]
    pallas_call x1, Pallas kernels: 10.2 us -> 8.28 us  [attend_block(): pl.pallas_call(attention_kernel, in_specs=[pl.BlockSpec(memory_space=pltp...]
    unnamed x12, local copies, waits for them, and re-layouts: 1.81 us -> 0.02 us
    all_to_all x1, blocking collectives: 27.8 us -> 26.2 us  [on_device(): parts = lax.all_to_all(parts, 'kv', split_axis=0, concat_axis=0, tiled=True)]
where the time goes in v2:
time: 99.8 us; the launch traced here: 99.4 us
  blocking collectives  81.8 us (82%)
  Pallas kernels  13.2 us (13%)
  waiting for transfers between devices  3.49 us (3%)
    all_to_all x1, blocking collectives, on_device(): parts = lax.all_to_all(parts, 'kv', split_axis=0, concat_axis=0, tiled=True)  26.2 us
    all_to_all x1, blocking collectives, on_device(): lax.all_to_all(summed, both, split_axis=0, concat_axis=0, tiled=True, axi...  17.5 us
    all_to_all x1, blocking collectives, on_device(): lax.all_to_all(spread, both, split_axis=0, concat_axis=0, tiled=True, axi...  16.4 us
    all_to_all x1, blocking collectives, on_device(): lax.all_to_all(projected, 'kv', split_axis=0, concat_axis=0, tiled=True)  11.2 us
    all_to_all x1, blocking collectives, on_device(): lax.all_to_all(head_values, 'ep', split_axis=0, concat_axis=0, tiled=True)  10.4 us
    pallas_call x1, Pallas kernels, attend_block(): pl.pallas_call(attention_kernel, in_specs=[pl.BlockSpec(memory_space=pltp...  8.28 us
    pallas_call x1, Pallas kernels, run_expert(): pl.pallas_call(expert_kernel, in_specs=[vmem] * 8, out_specs=(vmem, vmem)...  2.28 us
  transfers between devices with their start and end apart: 2, of which 2 were waited for; matrix products, arithmetic and copies ran while one was open for 0% of the time, Pallas kernels for 0%

profile of v2, /device:TPU:0, one launch (start us, length us, event | category | flops | bytes accessed | tf_op | source)
XLA Modules:
  0.0 99.4 jit_solution(10927855507178341763)
XLA Ops:
  0.6 0.0 copy-start.1
  0.6 8.3 %attend_block.1 = (bf16[16,72,512]{2,1,0:T(8,128)(2,1)S(1)}, bf16[7168,256]{1,0:T(8,128)(2,1)S(1)}, bf16[7168,256]{1,0:T(8,128)(2,1)S(1)}, bf16[256,7168]{1,0:T(8,128)(2,1)S(1)}) custom-call(s32[8]{0:T(128)} %lengths_ref.1, bf16[8,576,128]{2,1,0:T(8,128)(2,1)} %bitcast.19, bf16[8,576,1024]{2,1,0:T(8,128)(2,1)} %bitcast.15, bf16[7168,256]{1,0:T(8,128)(2,1)} %bitcast.16, ...), custom_call_target="tpu_custom_call" | custom-call | flops 2281701376 | bytes 10616832 | tf_op jit(solution)/shard_map/attend_block/pallas_call | solution.py:119
  8.9 26.2 %all_to_all.31.parts_ref = bf16[16,72,512]{2,1,0:T(8,128)(2,1)S(1)} all-to-all(bf16[16,72,512]{2,1,0:T(8,128)(2,1)S(1)} %get-tuple-element.10), channel_id=1, replica_groups=mesh['kv'=16,'ep'=8] {'kv'}, dimensions={0} | all-to-all | bytes 2359296 | tf_op jit(solution)/shard_map/all_to_all | solution.py:409
  35.2 0.0 copy-done.1
  35.2 0.0 copy-start
  35.2 0.6 merge_blocks.1
  35.7 10.4 %all_to_all.32 = bf16[8,8,1024]{2,1,0:T(8,128)(2,1)S(1)} all-to-all(bf16[8,8,1024]{2,1,0:T(8,128)(2,1)S(1)} %bitcast.10), channel_id=1, replica_groups=mesh['kv'=16,'ep'=8] {'ep'}, dimensions={0} | all-to-all | bytes 262144 | tf_op jit(solution)/shard_map/all_to_all | solution.py:411
  46.1 0.0 copy-done
  46.1 0.0 copy-start.3
  46.1 0.4 project.1
  46.6 11.2 %all_to_all.33.parts_ref = bf16[16,4,896]{2,1,0:T(4,128)(2,1)S(1)} all-to-all(bf16[16,4,896]{2,1,0:T(4,128)(2,1)S(1)} %project.1), channel_id=1, replica_groups=mesh['kv'=16,'ep'=8] {'kv'}, dimensions={0} | all-to-all | bytes 229376 | tf_op jit(solution)/shard_map/all_to_all | solution.py:414
  57.8 0.0 copy-done.3
  57.8 0.6 add_residual.1
  58.5 16.4 %all_to_all.34.parts_ref = bf16[64,4,896]{2,1,0:T(4,128)(2,1)S(1)} all-to-all(bf16[64,4,896]{2,1,0:T(4,128)(2,1)S(1)} %get-tuple-element.15), channel_id=1, replica_groups={{0,8,16,24,32,40,48,56,64,72,80,88,96,104,112,120,2,10,18,26,34,42,50,5..., dimensions={0} | all-to-all | bytes 917504 | tf_op jit(solution)/shard_map/all_to_all | solution.py:417
  74.9 0.0 copy-start.2
  74.9 0.0 copy-start.4
  74.9 0.0 copy-start.5
  74.9 0.1 regroup.1.mine_ref
  75.0 0.1 collective-permute-start
  75.1 1.8 %collective-permute-done.other_ref = bf16[4,64,896]{2,1,0:T(8,128)(2,1)S(1)} collective-permute-done((bf16[4,64,896]{2,1,0:T(8,128)(2,1)S(1)}, bf16[4,64,896]{2,1,0:T(8,128)(2,1)S(1)}, u32[]{:S(2)}, u32[]{:S(2)}) %collective-permute-start) | collective-permute-done | bytes 458784 | tf_op jit(solution)/shard_map/ppermute | solution.py:421
  76.9 0.0 copy-done.2
  76.9 0.0 copy-done.4
  76.9 0.0 copy-done.5
  76.9 2.3 %run_expert.1 = (bf16[4,64,896]{2,1,0:T(8,128)(2,1)S(1)}, bf16[4,64,896]{2,1,0:T(8,128)(2,1)S(1)}) custom-call(bf16[4,64,896]{2,1,0:T(8,128)(2,1)S(1)} %regroup.1.mine_ref, bf16[4,64,896]{2,1,0:T(8,128)(2,1)S(1)} %collective-permute-done.other_ref, f32[1,7168]{1,0:T(1,128)S(1)} %bitcast.12, s32[8,64]{1,0:T(8,128)S(1)} %bitcast.13, f32[8,64]{1,0:T(8,128)S(1)} %bitcast.14, ...), custom_call_target="tpu_custom_call" | custom-call | flops 704643072 | bytes 11010048 | tf_op jit(solution)/shard_map/run_expert/pallas_call | solution.py:298
  79.2 0.2 collective-permute-start.1
  79.4 1.7 %collective-permute-done.1.given_ref = bf16[4,64,896]{2,1,0:T(8,128)(2,1)S(1)} collective-permute-done((bf16[4,64,896]{2,1,0:T(8,128)(2,1)S(1)}, bf16[4,64,896]{2,1,0:T(8,128)(2,1)S(1)}, u32[]{:S(2)}, u32[]{:S(2)}) %collective-permute-start.1) | collective-permute-done | bytes 458784 | tf_op jit(solution)/shard_map/ppermute | solution.py:430
  81.1 0.1 add_pair.1
  81.2 17.5 %all_to_all.35.parts_ref = bf16[64,4,896]{2,1,0:T(4,128)(2,1)S(1)} all-to-all(bf16[64,4,896]{2,1,0:T(4,128)(2,1)S(1)} %add_pair.1), channel_id=1, replica_groups={{0,8,16,24,32,40,48,56,64,72,80,88,96,104,112,120,2,10,18,26,34,42,50,5..., dimensions={0} | all-to-all | bytes 917504 | tf_op jit(solution)/shard_map/all_to_all | solution.py:432
  98.8 0.7 add_total.1
Async XLA Ops:
  0.6 34.5 %copy-start.1 = (bf16[8,512,128]{2,1,0:T(8,128)(2,1)S(1)}, bf16[8,512,128]{2,1,0:T(8,128)(2,1)}, u32[]{:S(2)}) copy-start(bf16[8,512,128]{2,1,0:T(8,128)(2,1)} %value_ref.1) | copy-start | bytes 3145732
  35.2 11.0 %copy-start = (bf16[1024,896]{1,0:T(8,128)(2,1)S(1)}, bf16[1024,896]{1,0:T(8,128)(2,1)}, u32[]{:S(2)}) copy-start(bf16[1024,896]{1,0:T(8,128)(2,1)} %proj_ref.1) | copy-start | bytes 5505028
  46.1 11.7 %copy-start.3 = (bf16[4,896]{1,0:T(4,128)(2,1)S(1)}, bf16[4,896]{1,0:T(4,128)(2,1)}, u32[]{:S(2)}) copy-start(bf16[4,896]{1,0:T(4,128)(2,1)} %residual_ref.1) | copy-start | bytes 21508
  74.9 2.0 %copy-start.2 = (f32[7168]{0:T(1024)S(1)}, f32[7168]{0:T(1024)}, u32[]{:S(2)}) copy-start(f32[7168]{0:T(1024)} %param.18) | copy-start | bytes 86020
  74.9 2.0 %copy-start.4 = (s32[64,8]{0,1:T(8,128)S(1)}, s32[64,8]{0,1:T(8,128)}, u32[]{:S(2)}) copy-start(s32[64,8]{0,1:T(8,128)} %param.19) | copy-start | bytes 6148
  74.9 2.0 %copy-start.5 = (f32[64,8]{0,1:T(8,128)S(1)}, f32[64,8]{0,1:T(8,128)}, u32[]{:S(2)}) copy-start(f32[64,8]{0,1:T(8,128)} %param.20) | copy-start | bytes 6148
  75.0 1.9 %collective-permute-start = (bf16[4,64,896]{2,1,0:T(8,128)(2,1)S(1)}, bf16[4,64,896]{2,1,0:T(8,128)(2,1)S(1)}, u32[]{:S(2)}, u32[]{:S(2)}) collective-permute-start(bf16[4,64,896]{2,1,0:T(8,128)(2,1)S(1)} %regroup.1.mine_ref), channel_id=1, source_target_pairs={{0,1},{1,0},{2,3},{3,2},{4,5},{5,4},{6,7},{7,6},{8,9},{9,8},{10,11... | collective-permute-start | bytes 1376264 | tf_op jit(solution)/shard_map/ppermute | solution.py:421
  79.2 1.9 %collective-permute-start.1 = (bf16[4,64,896]{2,1,0:T(8,128)(2,1)S(1)}, bf16[4,64,896]{2,1,0:T(8,128)(2,1)S(1)}, u32[]{:S(2)}, u32[]{:S(2)}) collective-permute-start(bf16[4,64,896]{2,1,0:T(8,128)(2,1)S(1)} %get-tuple-element.17), channel_id=1, source_target_pairs={{0,1},{1,0},{2,3},{3,2},{4,5},{5,4},{6,7},{7,6},{8,9},{9,8},{10,11... | collective-permute-start | bytes 1376264 | tf_op jit(solution)/shard_map/ppermute | solution.py:430

commit v3 on v2

--- a/solution.py
+++ b/solution.py
@@ -223,7 +223,7 @@
     return pl.pallas_call(
         residual_kernel,
         out_shape=(
-            jax.ShapeDtypeStruct(residual.shape, jnp.bfloat16),
+            pltpu.VMEM(residual.shape, jnp.bfloat16),
             jax.ShapeDtypeStruct((copies,) + residual.shape, jnp.bfloat16),
         ),
         compiler_params=pltpu.CompilerParams(vmem_limit_bytes=8 * MIB),
@@ -234,29 +234,86 @@
     )(parts, residual, *held)
 
 
+def half_product(parts_ref, gain_ref, w_gate_ref, w_up_ref, core):
+    col_count = parts_ref.shape[2]
+    chips = gain_ref.shape[1] // (2 * col_count)
+    each = parts_ref.shape[0] // chips
+    row_count = each * parts_ref.shape[1]
+    squares = jnp.zeros((row_count, col_count), jnp.float32)
+    gate_act = jnp.zeros((row_count, w_gate_ref.shape[1]), jnp.float32)
+    up_act = gate_act
+    for y in range(chips):
+        at = pl.ds(pl.multiple_of((2 * y + core) * col_count, LANES), col_count)
+        wide = jnp.concatenate(
+            [parts_ref[y * each + k].astype(jnp.float32) for k in range(each)], axis=0
+        )
+        squares = squares + wide * wide
+        scaled = (wide * gain_ref[:, at]).astype(jnp.bfloat16)
+        gate_act = gate_act + jnp.dot(
+            scaled, w_gate_ref[at, :], preferred_element_type=jnp.float32
+        )
+        up_act = up_act + jnp.dot(scaled, w_up_ref[at, :], preferred_element_type=jnp.float32)
+    return gate_act, up_act, jnp.sum(squares, axis=1, keepdims=True)
+
+
+def own_half_kernel(mine_ref, gain_ref, w_gate_ref, w_up_ref, *refs):
+    gate_ref, up_ref, squares_ref = refs[-3:]
+    core = lax.rem(lax.axis_index("ep"), 2)
+    gate_act, up_act, squares = half_product(mine_ref, gain_ref, w_gate_ref, w_up_ref, core)
+    gate_ref[...] = gate_act
+    up_ref[...] = up_act
+    squares_ref[...] = jnp.broadcast_to(squares, squares_ref.shape)
+
+
+def run_own_half(mine, gain, w_gate, w_up, held):
+    row_count = mine.shape[0] * mine.shape[1] * 2 * mine.shape[2] // w_gate.shape[0]
+    width = w_gate.shape[1]
+    return pl.pallas_call(
+        own_half_kernel,
+        out_shape=(
+            jax.ShapeDtypeStruct((row_count, width), jnp.float32),
+            jax.ShapeDtypeStruct((row_count, width), jnp.float32),
+            jax.ShapeDtypeStruct((row_count, LANES), jnp.float32),
+        ),
+        compiler_params=pltpu.CompilerParams(vmem_limit_bytes=12 * MIB),
+        cost_estimate=pl.CostEstimate(
+            flops=2 * row_count * w_gate.size, bytes_accessed=2 * w_gate.size, transcendentals=0
+        ),
+        name="own_half",
+    )(mine, gain, w_gate, w_up, *held)
+
+
 def expert_kernel(
-    mine_ref,
     other_ref,
+    gate_ref,
+    up_ref,
+    squares_ref,
     gain_ref,
     ids_ref,
     gates_ref,
     w_gate_ref,
     w_up_ref,
     w_down_ref,
-    keep_ref,
+    attended_ref,
     give_ref,
-    normed_ref,
+    hidden_ref,
+    share_ref,
+    attended_hbm,
+    sent,
 ):
-    chips, row_count, col_count = mine_ref.shape
-    full_width = normed_ref.shape[1]
+    save = pltpu.make_async_copy(attended_ref, attended_hbm, sent)
+    save.start()
+    chips, row_count, col_count = give_ref.shape
+    full_width = gain_ref.shape[1]
     expert = lax.axis_index("kv")
-    first = lax.rem(lax.axis_index("ep"), 2) == 0
-    squares = jnp.zeros((row_count, col_count), jnp.float32)
-    for y in range(chips):
-        for piece in (mine_ref[y], other_ref[y]):
-            wide = piece.astype(jnp.float32)
-            squares = squares + wide * wide
-    inverse = lax.rsqrt(jnp.sum(squares, axis=1, keepdims=True) / full_width + NORM_EPS)
+    other = 1 - lax.rem(lax.axis_index("ep"), 2)
+    gate_act, up_act, squares = half_product(other_ref, gain_ref, w_gate_ref, w_up_ref, other)
+    squares = squares + squares_ref[:, :1]
+    inverse = lax.rsqrt(squares / full_width + NORM_EPS)
+    gate_act = (gate_act + gate_ref[...]) * inverse
+    up_act = (up_act + up_ref[...]) * inverse
+    hidden = (gate_act / (1.0 + jnp.exp(-gate_act)) * up_act).astype(jnp.bfloat16)
+    hidden_ref[...] = hidden
     chosen = jnp.where(ids_ref[...] == expert, gates_ref[...], 0.0)
     in_lanes = jnp.sum(chosen, axis=0, keepdims=True)
     square = (row_count, row_count)
@@ -264,51 +321,61 @@
         jnp.int32, square, 1
     )
     row_gate = jnp.sum(jnp.where(same, in_lanes, 0.0), axis=1, keepdims=True)
+    share_ref[...] = jnp.broadcast_to(row_gate, share_ref.shape)
     for y in range(chips):
-        mine = mine_ref[y].astype(jnp.float32)
-        other = other_ref[y].astype(jnp.float32)
-        for c, piece in enumerate(
-            (jnp.where(first, mine, other), jnp.where(first, other, mine))
-        ):
-            cols = slice((2 * y + c) * col_count, (2 * y + c + 1) * col_count)
-            normed_ref[:, cols] = (piece * inverse * gain_ref[:, cols]).astype(jnp.bfloat16)
-    normed = normed_ref[...]
-    gate_act = jnp.dot(normed, w_gate_ref[...], preferred_element_type=jnp.float32)
-    up_act = jnp.dot(normed, w_up_ref[...], preferred_element_type=jnp.float32)
-    hidden = (gate_act / (1.0 + jnp.exp(-gate_act)) * up_act).astype(jnp.bfloat16)
+        at = pl.ds(pl.multiple_of((2 * y + other) * col_count, LANES), col_count)
+        terms = jnp.dot(hidden, w_down_ref[:, at], preferred_element_type=jnp.float32)
+        give_ref[y] = (terms * row_gate).astype(jnp.bfloat16)
+    save.wait()
+
+
+def run_expert(other, gate, up, squares, gain, ids, gates, w_gate, w_up, w_down, attended):
+    row_count, hidden_width = gate.shape
+    full_width = w_gate.shape[0]
+    chips = full_width // (2 * other.shape[2])
+    vmem = pl.BlockSpec(memory_space=pltpu.VMEM)
+    return pl.pallas_call(
+        expert_kernel,
+        in_specs=[vmem] * 11,
+        out_specs=(vmem, vmem, vmem, pl.BlockSpec(memory_space=pltpu.HBM)),
+        out_shape=(
+            jax.ShapeDtypeStruct((chips, row_count, other.shape[2]), jnp.bfloat16),
+            jax.ShapeDtypeStruct((row_count, hidden_width), jnp.bfloat16),
+            jax.ShapeDtypeStruct((row_count, LANES), jnp.float32),
+            jax.ShapeDtypeStruct(attended.shape, attended.dtype),
+        ),
+        scratch_shapes=[pltpu.SemaphoreType.DMA],
+        compiler_params=pltpu.CompilerParams(vmem_limit_bytes=12 * MIB),
+        cost_estimate=pl.CostEstimate(
+            flops=4 * row_count * full_width * hidden_width,
+            bytes_accessed=4 * full_width * hidden_width,
+            transcendentals=row_count * hidden_width,
+        ),
+        name="run_expert",
+    )(other, gate, up, squares, gain, ids, gates, w_gate, w_up, w_down, attended)
+
+
+def keep_kernel(hidden_ref, share_ref, w_down_ref, keep_ref):
+    chips, unused_rows, col_count = keep_ref.shape
+    core = lax.rem(lax.axis_index("ep"), 2)
+    hidden = hidden_ref[...]
+    row_gate = share_ref[:, :1]
     for y in range(chips):
-        both = [
-            jnp.dot(
-                hidden,
-                w_down_ref[:, (2 * y + c) * col_count : (2 * y + c + 1) * col_count],
-                preferred_element_type=jnp.float32,
-            )
-            * row_gate
-            for c in range(2)
-        ]
-        keep_ref[y] = jnp.where(first, both[0], both[1]).astype(jnp.bfloat16)
-        give_ref[y] = jnp.where(first, both[1], both[0]).astype(jnp.bfloat16)
-
-
-def run_expert(mine, other, gain, ids, gates, w_gate, w_up, w_down):
-    row_count = mine.shape[1]
-    full_width, hidden_width = w_gate.shape
-    vmem = pl.BlockSpec(memory_space=pltpu.VMEM)
-    half = jax.ShapeDtypeStruct(mine.shape, jnp.bfloat16)
-    return pl.pallas_call(
-        expert_kernel,
-        in_specs=[vmem] * 8,
-        out_specs=(vmem, vmem),
-        out_shape=(half, half),
-        scratch_shapes=[pltpu.VMEM((row_count, full_width), jnp.bfloat16)],
+        at = pl.ds(pl.multiple_of((2 * y + core) * col_count, LANES), col_count)
+        terms = jnp.dot(hidden, w_down_ref[:, at], preferred_element_type=jnp.float32)
+        keep_ref[y] = (terms * row_gate).astype(jnp.bfloat16)
+
+
+def run_keep(hidden, share, w_down, like):
+    return pl.pallas_call(
+        keep_kernel,
+        out_shape=jax.ShapeDtypeStruct(like.shape, like.dtype),
         compiler_params=pltpu.CompilerParams(vmem_limit_bytes=12 * MIB),
         cost_estimate=pl.CostEstimate(
-            flops=6 * row_count * full_width * hidden_width,
-            bytes_accessed=6 * full_width * hidden_width,
-            transcendentals=row_count * hidden_width,
-        ),
-        name="run_expert",
-    )(mine, other, gain, ids, gates, w_gate, w_up, w_down)
+            flops=hidden.shape[0] * w_down.size, bytes_accessed=w_down.size, transcendentals=0
+        ),
+        name="run_keep",
+    )(hidden, share, w_down)
 
 
 def pair_kernel(keep_ref, given_ref, out_ref):
@@ -342,26 +409,6 @@
     for k in range(1, parts_ref.shape[0]):
         total = total + parts_ref[k].astype(jnp.float32)
     out_ref[...] = total.astype(jnp.bfloat16)
-
-
-def regroup_kernel(parts_ref, *refs):
-    out_ref = refs[-1]
-    chips = out_ref.shape[0]
-    each = parts_ref.shape[0] // chips
-    for y in range(chips):
-        out_ref[y] = jnp.concatenate(
-            [parts_ref[y * each + k].astype(jnp.float32) for k in range(each)], axis=0
-        ).astype(jnp.bfloat16)
-
-
-def regroup(parts, chips, held):
-    count, rows, cols = parts.shape
-    return pl.pallas_call(
-        regroup_kernel,
-        out_shape=jax.ShapeDtypeStruct((chips, count // chips * rows, cols), jnp.bfloat16),
-        compiler_params=pltpu.CompilerParams(vmem_limit_bytes=8 * MIB),
-        name="regroup",
-    )(parts, *held)
 
 
 def add_total(parts):
@@ -417,17 +464,15 @@
     mine = lax.all_to_all(
         spread, both, split_axis=0, concat_axis=0, tiled=True, axis_index_groups=same_core
     )
-    mine = regroup(mine, chips, weights)
     other = lax.ppermute(mine, "ep", other_core)
-    keep, give = run_expert(
-        mine,
-        other,
-        norm_gain[None],
-        route_ids.T,
-        route_gates.T,
-        *weights,
+    gain = norm_gain[None]
+    w_gate, w_up, w_down = weights
+    partial = run_own_half(mine, gain, w_gate, w_up, [w_down])
+    give, hidden, share, attended = run_expert(
+        other, *partial, gain, route_ids.T, route_gates.T, w_gate, w_up, w_down, attended
     )
     given = lax.ppermute(give, "ep", other_core)
+    keep = run_keep(hidden, share, w_down, give)
     summed = add_pair(keep, given, own_rows)
     arrived = lax.all_to_all(
         summed, both, split_axis=0, concat_axis=0, tiled=True, axis_index_groups=same_core

time: 99.8 us -> 98.4 us (0.986)
  waiting for transfers between devices: 3.49 us -> 2.28 us
    pallas_call x3 -> x4, Pallas kernels: 3.03 us -> 2.88 us  [the longest x1 1.64 us: run_expert(): pl.pallas_call(expert_kernel, in_specs=[vmem] * 11, out_specs=(vmem, vmem...]
  transfers between devices with their start and end apart: 2 -> 2, of which waited for: 2 -> 2; matrix products, arithmetic and copies ran while one was open for 0% -> 0% of each run, Pallas kernels for 0% -> 1%
where the time goes in v3:
time: 98.4 us; the launch traced here: 98 us
  blocking collectives  81.8 us (83%)
  Pallas kernels  13 us (13%)
  waiting for transfers between devices  2.28 us (2%)
    all_to_all x1, blocking collectives, on_device(): parts = lax.all_to_all(parts, 'kv', split_axis=0, concat_axis=0, tiled=True)  26.2 us
    all_to_all x1, blocking collectives, on_device(): lax.all_to_all(summed, both, split_axis=0, concat_axis=0, tiled=True, axi...  17.5 us
    all_to_all x1, blocking collectives, on_device(): lax.all_to_all(spread, both, split_axis=0, concat_axis=0, tiled=True, axi...  16.4 us
    all_to_all x1, blocking collectives, on_device(): lax.all_to_all(projected, 'kv', split_axis=0, concat_axis=0, tiled=True)  11.2 us
    all_to_all x1, blocking collectives, on_device(): lax.all_to_all(head_values, 'ep', split_axis=0, concat_axis=0, tiled=True)  10.4 us
    pallas_call x1, Pallas kernels, attend_block(): pl.pallas_call(attention_kernel, in_specs=[pl.BlockSpec(memory_space=pltp...  8.28 us
  transfers between devices with their start and end apart: 2, of which 2 were waited for; matrix products, arithmetic and copies ran while one was open for 0% of the time, Pallas kernels for 1%

profile of v3, /device:TPU:0, one launch (start us, length us, event | category | flops | bytes accessed | tf_op | source)
XLA Modules:
  0.0 98.0 jit_solution(8377659992671719869)
XLA Ops:
  0.6 0.0 copy-start.1
  0.6 8.3 %attend_block.1 = (bf16[16,72,512]{2,1,0:T(8,128)(2,1)S(1)}, bf16[7168,256]{1,0:T(8,128)(2,1)S(1)}, bf16[7168,256]{1,0:T(8,128)(2,1)S(1)}, bf16[256,7168]{1,0:T(8,128)(2,1)S(1)}) custom-call(s32[8]{0:T(128)} %lengths_ref.1, bf16[8,576,128]{2,1,0:T(8,128)(2,1)} %bitcast.20, bf16[8,576,1024]{2,1,0:T(8,128)(2,1)} %bitcast.16, bf16[7168,256]{1,0:T(8,128)(2,1)} %bitcast.17, ...), custom_call_target="tpu_custom_call" | custom-call | flops 2281701376 | bytes 10616832 | tf_op jit(solution)/shard_map/attend_block/pallas_call | solution.py:119
  8.9 26.2 %all_to_all.31.parts_ref = bf16[16,72,512]{2,1,0:T(8,128)(2,1)S(1)} all-to-all(bf16[16,72,512]{2,1,0:T(8,128)(2,1)S(1)} %get-tuple-element.15), channel_id=1, replica_groups=mesh['kv'=16,'ep'=8] {'kv'}, dimensions={0} | all-to-all | bytes 2359296 | tf_op jit(solution)/shard_map/all_to_all | solution.py:456
  35.2 0.0 copy-done.1
  35.2 0.0 copy-start
  35.2 0.6 merge_blocks.1
  35.7 10.4 %all_to_all.32 = bf16[8,8,1024]{2,1,0:T(8,128)(2,1)S(1)} all-to-all(bf16[8,8,1024]{2,1,0:T(8,128)(2,1)S(1)} %bitcast.10), channel_id=1, replica_groups=mesh['kv'=16,'ep'=8] {'ep'}, dimensions={0} | all-to-all | bytes 262144 | tf_op jit(solution)/shard_map/all_to_all | solution.py:458
  46.1 0.0 copy-done
  46.1 0.0 copy-start.3
  46.1 0.4 project.1
  46.6 11.2 %all_to_all.33.parts_ref = bf16[16,4,896]{2,1,0:T(4,128)(2,1)S(1)} all-to-all(bf16[16,4,896]{2,1,0:T(4,128)(2,1)S(1)} %project.1), channel_id=1, replica_groups=mesh['kv'=16,'ep'=8] {'kv'}, dimensions={0} | all-to-all | bytes 229376 | tf_op jit(solution)/shard_map/all_to_all | solution.py:461
  57.8 0.0 copy-done.3
  57.8 0.0 copy-start.2
  57.8 0.1 add_residual.1
  57.9 16.4 %all_to_all.34.mine_ref = bf16[64,4,896]{2,1,0:T(4,128)(2,1)S(1)} all-to-all(bf16[64,4,896]{2,1,0:T(4,128)(2,1)S(1)} %get-tuple-element.19), channel_id=1, replica_groups={{0,8,16,24,32,40,48,56,64,72,80,88,96,104,112,120,2,10,18,26,34,42,50,5..., dimensions={0} | all-to-all | bytes 917504 | tf_op jit(solution)/shard_map/all_to_all | solution.py:464
  74.3 0.0 collective-permute-start
  74.3 0.0 copy-done.2
  74.3 0.0 copy-start.4
  74.3 0.0 copy-start.5
  74.3 0.8 own_half.1
  75.1 1.0 %collective-permute-done.other_ref = bf16[64,4,896]{2,1,0:T(4,128)(2,1)S(1)} collective-permute-done((bf16[64,4,896]{2,1,0:T(4,128)(2,1)S(1)}, bf16[64,4,896]{2,1,0:T(4,128)(2,1)S(1)}, u32[]{:S(2)}, u32[]{:S(2)}) %collective-permute-start) | collective-permute-done | bytes 458784 | tf_op jit(solution)/shard_map/ppermute | solution.py:467
  76.1 0.0 copy-done.4
  76.1 0.0 copy-done.5
  76.1 1.6 %run_expert.1 = (bf16[4,64,896]{2,1,0:T(8,128)(2,1)S(1)}, bf16[64,256]{1,0:T(8,128)(2,1)S(1)}, f32[64,128]{1,0:T(8,128)S(1)}, bf16[4,896]{1,0:T(4,128)(2,1)}) custom-call(bf16[64,4,896]{2,1,0:T(4,128)(2,1)S(1)} %collective-permute-done.other_ref, f32[64,256]{1,0:T(8,128)S(1)} %get-tuple-element.20.gate_ref, f32[64,256]{1,0:T(8,128)S(1)} %get-tuple-element.21.up_ref, ...), custom_call_target="tpu_custom_call" | custom-call | flops 469762048 | bytes 7340032 | tf_op jit(solution)/shard_map/run_expert/pallas_call | solution.py:337
  77.8 0.2 collective-permute-start.1
  78.0 0.4 run_keep.1.keep_ref
  78.4 1.3 %collective-permute-done.1.given_ref = bf16[4,64,896]{2,1,0:T(8,128)(2,1)S(1)} collective-permute-done((bf16[4,64,896]{2,1,0:T(8,128)(2,1)S(1)}, bf16[4,64,896]{2,1,0:T(8,128)(2,1)S(1)}, u32[]{:S(2)}, u32[]{:S(2)}) %collective-permute-start.1) | collective-permute-done | bytes 458784 | tf_op jit(solution)/shard_map/ppermute | solution.py:474
  79.7 0.1 add_pair.1
  79.8 17.5 %all_to_all.35.parts_ref = bf16[64,4,896]{2,1,0:T(4,128)(2,1)S(1)} all-to-all(bf16[64,4,896]{2,1,0:T(4,128)(2,1)S(1)} %add_pair.1), channel_id=1, replica_groups={{0,8,16,24,32,40,48,56,64,72,80,88,96,104,112,120,2,10,18,26,34,42,50,5..., dimensions={0} | all-to-all | bytes 917504 | tf_op jit(solution)/shard_map/all_to_all | solution.py:477
  97.3 0.7 add_total.1
Async XLA Ops:
  0.6 34.5 %copy-start.1 = (bf16[8,512,128]{2,1,0:T(8,128)(2,1)S(1)}, bf16[8,512,128]{2,1,0:T(8,128)(2,1)}, u32[]{:S(2)}) copy-start(bf16[8,512,128]{2,1,0:T(8,128)(2,1)} %value_ref.1) | copy-start | bytes 3145732
  35.2 11.0 %copy-start = (bf16[1024,896]{1,0:T(8,128)(2,1)S(1)}, bf16[1024,896]{1,0:T(8,128)(2,1)}, u32[]{:S(2)}) copy-start(bf16[1024,896]{1,0:T(8,128)(2,1)} %proj_ref.1) | copy-start | bytes 5505028
  46.1 11.7 %copy-start.3 = (bf16[4,896]{1,0:T(4,128)(2,1)S(1)}, bf16[4,896]{1,0:T(4,128)(2,1)}, u32[]{:S(2)}) copy-start(bf16[4,896]{1,0:T(4,128)(2,1)} %residual_ref.1) | copy-start | bytes 21508
  57.8 16.5 %copy-start.2 = (f32[7168]{0:T(1024)S(1)}, f32[7168]{0:T(1024)}, u32[]{:S(2)}) copy-start(f32[7168]{0:T(1024)} %param.18) | copy-start | bytes 86020
  74.3 1.8 %collective-permute-start = (bf16[64,4,896]{2,1,0:T(4,128)(2,1)S(1)}, bf16[64,4,896]{2,1,0:T(4,128)(2,1)S(1)}, u32[]{:S(2)}, u32[]{:S(2)}) collective-permute-start(bf16[64,4,896]{2,1,0:T(4,128)(2,1)S(1)} %all_to_all.34.mine_ref), channel_id=1, source_target_pairs={{0,1},{1,0},{2,3},{3,2},{4,5},{5,4},{6,7},{7,6},{8,9},{9,8},{10,11... | collective-permute-start | bytes 1376264 | tf_op jit(solution)/shard_map/ppermute | solution.py:467
  74.3 1.8 %copy-start.4 = (s32[64,8]{0,1:T(8,128)S(1)}, s32[64,8]{0,1:T(8,128)}, u32[]{:S(2)}) copy-start(s32[64,8]{0,1:T(8,128)} %param.19) | copy-start | bytes 6148
  74.3 1.8 %copy-start.5 = (f32[64,8]{0,1:T(8,128)S(1)}, f32[64,8]{0,1:T(8,128)}, u32[]{:S(2)}) copy-start(f32[64,8]{0,1:T(8,128)} %param.20) | copy-start | bytes 6148
  77.8 1.9 %collective-permute-start.1 = (bf16[4,64,896]{2,1,0:T(8,128)(2,1)S(1)}, bf16[4,64,896]{2,1,0:T(8,128)(2,1)S(1)}, u32[]{:S(2)}, u32[]{:S(2)}) collective-permute-start(bf16[4,64,896]{2,1,0:T(8,128)(2,1)S(1)} %get-tuple-element.27), channel_id=1, source_target_pairs={{0,1},{1,0},{2,3},{3,2},{4,5},{5,4},{6,7},{7,6},{8,9},{9,8},{10,11... | collective-permute-start | bytes 1376264 | tf_op jit(solution)/shard_map/ppermute | solution.py:474
